TPU v7x, 32 devices: a whole 2x2x4 slice. The times are simulated.
32 devices in a mesh: gz: 4 (over x, core), xy: 8 (over z, y).
Axes of the slice: x: 2, y: 2, z: 4, core: 2. Of those that a mesh axis runs over, the one named last changes fastest.
Arguments:
- adjoint_e: float32 [3, 56, 128, 128], P(None, 'gz', 'xy'), may hold values from -6 to 6
- adjoint_h: float32 [3, 56, 128, 128], P(None, 'gz', 'xy'), may hold values from -6 to 6
- source_e: bfloat16 [3, 56, 128, 128], P(None, 'gz', 'xy'), may hold values from -6 to 6
- e_saved: bfloat16 [3, 3, 56, 128, 128], P(None, None, 'gz', 'xy'), may hold values from -6 to 6
- material_eps: float32 [8], replicated, may hold values from 1 to 12
- material_id: int32 [56, 128, 128], P('gz', 'xy'), may hold values from 0 to 7
- pml_level: int32 [56, 128, 128], P('gz', 'xy'), may hold values from 0 to 3
- block_map: int32 [128, 128], P('xy'), may hold values from 0 to 64, as said below
Outputs:
- field_e: float32 [3, 56, 128, 128], P(None, 'gz', 'xy')
- field_h: float32 [3, 56, 128, 128], P(None, 'gz', 'xy')
- design_grad: float32 [64], P(('gz', 'xy'))
Inputs may be any that keep to these rules, and one draw needn't show every extreme that they name: block_map is constant over aligned groups of 4 x 4 columns; every value from 0 to 64 occurs.
All inputs are finite; a program needn't handle non-finite values.
Results may differ from a plain program's by a relative error of at most 0.0004.
Values sent between devices are 32-bit elements; how exact they have to be, the bound alone decides.
No kernel may reach another device: no remote copies, remote signals or barrier semaphores. Data moves between devices by JAX's collectives and lax.ppermute only.
A program may use at most 64 MiB of HBM per device.

v0:
```python
import jax
import jax.numpy as jnp
from jax import lax
from jax.sharding import PartitionSpec as P

B_DEV = 2


DT_STEP = 0.5
SIGMA_UNIT = 0.15


def shifted(value, axis, steps):
    count = lax.axis_size(axis)
    leading, last = (max(0, -steps), min(count, count - steps))
    return lax.ppermute(value, axis, [(source, source + steps) for source in range(leading, last)])


def step_next(field, axis):
    count = field.shape[axis]
    upper = lax.slice_in_dim(field, 1, count, axis=axis)
    zero_row = jnp.zeros_like(lax.slice_in_dim(field, 0, 1, axis=axis))
    return jnp.concatenate([upper, zero_row], axis=axis) - field


def step_prev(field, axis):
    count = field.shape[axis]
    lower = lax.slice_in_dim(field, 0, count - 1, axis=axis)
    zero_row = jnp.zeros_like(lax.slice_in_dim(field, 0, 1, axis=axis))
    return field - jnp.concatenate([zero_row, lower], axis=axis)


def curl_from(along_z, along_x, along_y):
    out_x = along_y[2] - along_z[1]
    out_y = along_z[0] - along_x[2]
    out_z = along_x[1] - along_y[0]
    return jnp.stack([out_x, out_y, out_z], 0)


def curl_next(field):
    rim_z = shifted(field[:, :1], "gz", -1)
    rim_x = shifted(field[:, :, :1], "xy", -1)
    along_z = jnp.concatenate([field[:, 1:], rim_z], 1) - field
    along_x = jnp.concatenate([field[:, :, 1:], rim_x], 2) - field
    along_y = step_next(field, 3)
    return curl_from(along_z, along_x, along_y)


def curl_prev(field):
    rim_z = shifted(field[:, -1:], "gz", 1)
    rim_x = shifted(field[:, :, -1:], "xy", 1)
    along_z = field - jnp.concatenate([rim_z, field[:, :-1]], 1)
    along_x = field - jnp.concatenate([rim_x, field[:, :, :-1]], 2)
    along_y = step_prev(field, 3)
    return curl_from(along_z, along_x, along_y)


def on_device(
    adjoint_e, adjoint_h, source_e, e_saved, material_eps, material_id, pml_level, block_map
):
    permit = jnp.zeros(material_id.shape, jnp.float32)
    for entry in range(material_eps.shape[0]):
        permit = permit + jnp.where(material_id == entry, material_eps[entry], 0.0)
    sigma = SIGMA_UNIT * pml_level.astype(jnp.float32)
    decay = (1.0 - sigma) / (1.0 + sigma)
    drive = DT_STEP / (permit * (1.0 + sigma))
    source = source_e.astype(jnp.float32)
    cell_grad = jnp.zeros(permit.shape, jnp.float32)
    field_e = adjoint_e
    field_h = adjoint_h
    for section in range(2):
        incoming = field_e + source
        after = e_saved[2 - section].astype(jnp.float32)
        before = e_saved[1 - section].astype(jnp.float32)
        cell_grad = cell_grad - jnp.sum(incoming * (after - decay * before), 0) / permit
        field_h = field_h + curl_next(drive * incoming)
        field_e = decay * incoming - DT_STEP * curl_prev(field_h)
    columns = jnp.sum(cell_grad, 0) / (cell_grad.shape[0] * lax.axis_size("gz"))
    blocks = B_DEV * lax.axis_size("gz") * lax.axis_size("xy")
    partial_sums = jax.ops.segment_sum(
        columns.reshape(-1), block_map.reshape(-1), num_segments=blocks + 1
    )[:blocks]
    design_grad = lax.psum_scatter(partial_sums, ("gz", "xy"), scatter_dimension=0, tiled=True)
    return (field_e, field_h, design_grad)


def solution(mesh):
    placed = (
        P(None, "gz", "xy", None),
        P(None, "gz", "xy", None),
        P(None, "gz", "xy", None),
        P(None, None, "gz", "xy", None),
        P(),
        P("gz", "xy", None),
        P("gz", "xy", None),
        P("xy", None),
    )
    return jax.shard_map(
        on_device,
        mesh=mesh,
        in_specs=placed,
        out_specs=(P(None, "gz", "xy", None), P(None, "gz", "xy", None), P(("gz", "xy"))),
        check_vma=False,
    )
```

profile of v0, /device:TPU:0, one launch (start us, length us, event | category | flops | bytes accessed | tf_op | source)
XLA Modules:
  0.0 103.5 jit_solution(9408587444395675892)
XLA Ops:
  0.6 1.6 %fusion.10 = (f32[1]{0:T(128)}, f32[1]{0:T(128)}, f32[1]{0:T(128)}, f32[1]{0:T(128)}, f32[1]{0:T(128)}, /*index=5*/f32[1]{0:T(128)}, f32[1]{0:T(128)}, f32[1]{0:T(128)}) fusion(f32[8]{0:T(128)} %param.12), kind=kLoop, calls=%fused_computation.52 | loop fusion | bytes 64 | tf_op jit(solution)/shard_map/slice | solution.py:63
  2.3 6.1 %subtract_divide_fusion = (f32[14,16,128]{2,1,0:T(8,128)S(1)}, f32[14,16,128]{2,1,0:T(8,128)S(1)}) fusion(s32[14,16,128]{2,1,0:T(8,128)} %param.14, f32[]{:T(128)} %bitcast.7, s32[14,16,128]{2,1,0:T(8,128)} %param.13, f32[]{:T(128)} %bitcast.6, f32[]{:T(128)} %bitcast.5, f32[]{:T(128)} %bitcast.4, f32[]{:T(128)} %bitcast.3, f32[]{:T(128)} %bitcast.2, ...), kind=kLoop, calls=%fused_computation.46 | loop fusion | flops 860160 | bytes 458784 | tf_op jit(solution)/shard_map/div | solution.py:65
  8.4 1.0 broadcast_multiply_fusion.1
  9.3 1.3 %collective-permute-start = (f32[3,1,16,128]{3,2,1,0:T(8,128)S(1)}, f32[3,1,16,128]{3,2,1,0:T(8,128)S(1)}, u32[]{:S(2)}, u32[]{:S(2)}) collective-permute-start(f32[3,1,16,128]{3,2,1,0:T(8,128)S(1)} %slice.228), channel_id=1, source_target_pairs={{8,0},{16,8},{24,16},{9,1},{17,9},{25,17},{10,2},{18,10},{26,18},{... | collective-permute-start | bytes 73736 | tf_op jit(solution)/shard_map/ppermute | solution.py:16
  10.7 1.3 %collective-permute-start.1 = (f32[3,14,1,128]{3,2,1,0:T(1,128)S(1)}, f32[3,14,1,128]{3,2,1,0:T(1,128)S(1)}, u32[]{:S(2)}, u32[]{:S(2)}) collective-permute-start(f32[3,14,1,128]{3,2,1,0:T(1,128)S(1)} %slice.232), channel_id=1, source_target_pairs={{1,0},{2,1},{3,2},{4,3},{5,4},{6,5},{7,6},{9,8},{10,9},{11,10},{12... | collective-permute-start | bytes 64520 | tf_op jit(solution)/shard_map/ppermute | solution.py:16
  12.0 0.1 slice.225
  12.2 5.1 %collective-permute-done.1 = f32[3,14,1,128]{3,2,1,0:T(1,128)S(1)} collective-permute-done((f32[3,14,1,128]{3,2,1,0:T(1,128)S(1)}, f32[3,14,1,128]{3,2,1,0:T(1,128)S(1)}, u32[]{:S(2)}, u32[]{:S(2)}) %collective-permute-start.1) | collective-permute-done | bytes 21536 | tf_op jit(solution)/shard_map/ppermute | solution.py:16
  17.3 0.1 maximum_subtract_fusion
  17.4 0.1 slice_subtract_fusion.11
  17.5 0.9 copy-done.1
  18.5 2.2 %collective-permute-start.2 = (f32[3,1,16,128]{3,2,1,0:T(8,128)S(1)}, f32[3,1,16,128]{3,2,1,0:T(8,128)S(1)}, u32[]{:S(2)}, u32[]{:S(2)}) collective-permute-start(f32[3,1,16,128]{3,2,1,0:T(8,128)S(1)} %slice.238), channel_id=1, source_target_pairs={{0,8},{8,16},{16,24},{1,9},{9,17},{17,25},{2,10},{10,18},{18,26},{... | collective-permute-start | bytes 73736 | tf_op jit(solution)/shard_map/ppermute | solution.py:16
  20.7 4.7 %collective-permute-start.3 = (f32[3,14,1,128]{3,2,1,0:T(1,128)S(1)}, f32[3,14,1,128]{3,2,1,0:T(1,128)S(1)}, u32[]{:S(2)}, u32[]{:S(2)}) collective-permute-start(f32[3,14,1,128]{3,2,1,0:T(1,128)S(1)} %slice.242), channel_id=1, source_target_pairs={{0,1},{1,2},{2,3},{3,4},{4,5},{5,6},{6,7},{8,9},{9,10},{10,11},{11... | collective-permute-start | bytes 64520 | tf_op jit(solution)/shard_map/ppermute | solution.py:16
  25.5 1.4 %collective-permute-done.3 = f32[3,14,1,128]{3,2,1,0:T(1,128)S(1)} collective-permute-done((f32[3,14,1,128]{3,2,1,0:T(1,128)S(1)}, f32[3,14,1,128]{3,2,1,0:T(1,128)S(1)}, u32[]{:S(2)}, u32[]{:S(2)}) %collective-permute-start.3) | collective-permute-done | bytes 21536 | tf_op jit(solution)/shard_map/ppermute | solution.py:16
  26.9 0.2 maximum_subtract_fusion.2
  27.1 0.0 copy-start.4
  27.2 0.8 copy-done.3
  28.0 0.2 copy-done.4
  28.2 0.2 fusion.2
  28.5 1.3 %collective-permute-start.5 = (f32[3,14,1,128]{3,2,1,0:T(1,128)S(1)}, f32[3,14,1,128]{3,2,1,0:T(1,128)S(1)}, u32[]{:S(2)}, u32[]{:S(2)}) collective-permute-start(f32[3,14,1,128]{3,2,1,0:T(1,128)S(1)} %slice.254), channel_id=1, source_target_pairs={{1,0},{2,1},{3,2},{4,3},{5,4},{6,5},{7,6},{9,8},{10,9},{11,10},{12... | collective-permute-start | bytes 64520 | tf_op jit(solution)/shard_map/ppermute | solution.py:16
  29.8 1.3 %collective-permute-start.4 = (f32[3,1,16,128]{3,2,1,0:T(8,128)S(1)}, f32[3,1,16,128]{3,2,1,0:T(8,128)S(1)}, u32[]{:S(2)}, u32[]{:S(2)}) collective-permute-start(f32[3,1,16,128]{3,2,1,0:T(8,128)S(1)} %slice.250), channel_id=1, source_target_pairs={{8,0},{16,8},{24,16},{9,1},{17,9},{25,17},{10,2},{18,10},{26,18},{... | collective-permute-start | bytes 73736 | tf_op jit(solution)/shard_map/ppermute | solution.py:16
  31.1 5.1 %subtract_reduce_fusion = f32[16,128]{1,0:T(8,128)S(1)} fusion(f32[14,16,128]{2,1,0:T(8,128)S(1)} %get-tuple-element.4, f32[14,16,128]{2,1,0:T(8,128)S(1)} %get-tuple-element.3, f32[]{:T(128)} %bitcast.7, s32[14,16,128]{2,1,0:T(8,128)S(1)} %copy-done.5, f32[]{:T(128)} %bitcast.6, f32[]{:T(128)} %bitcast.5, f32[]{:T(128)} %bitcast.4, f32[]{:T(128)} %bitcast.3, ...), kind=kLoop, calls=%fused_computation.43 | loop fusion | flops 800768 | bytes 352288 | tf_op jit(solution)/shard_map/reduce_sum | solution.py:78
  36.3 0.1 slice.247
  36.5 0.1 maximum_subtract_fusion.4
  36.7 0.1 maximum_add_fusion.1
  36.8 0.0 copy-start
  36.8 4.8 %collective-permute-start.7 = (f32[3,14,1,128]{3,2,1,0:T(1,128)S(1)}, f32[3,14,1,128]{3,2,1,0:T(1,128)S(1)}, u32[]{:S(2)}, u32[]{:S(2)}) collective-permute-start(f32[3,14,1,128]{3,2,1,0:T(1,128)S(1)} %slice.264), channel_id=1, source_target_pairs={{0,1},{1,2},{2,3},{3,4},{4,5},{5,6},{6,7},{8,9},{9,10},{10,11},{11... | collective-permute-start | bytes 64520 | tf_op jit(solution)/shard_map/ppermute | solution.py:16
  41.7 3.2 %collective-permute-start.6 = (f32[3,1,16,128]{3,2,1,0:T(8,128)S(1)}, f32[3,1,16,128]{3,2,1,0:T(8,128)S(1)}, u32[]{:S(2)}, u32[]{:S(2)}) collective-permute-start(f32[3,1,16,128]{3,2,1,0:T(8,128)S(1)} %slice.260), channel_id=1, source_target_pairs={{0,8},{8,16},{16,24},{1,9},{9,17},{17,25},{2,10},{10,18},{18,26},{... | collective-permute-start | bytes 73736 | tf_op jit(solution)/shard_map/ppermute | solution.py:16
  44.9 14.8 %scatter_custom_fusion = f32[65]{0:T(128)S(1)} fusion(s32[2048]{0:T(1024)} %bitcast.30, f32[2048]{0:T(1024)S(1)} %multiply_bitcast_fusion, f32[]{:T(128)} %constant.1.clone.1), kind=kCustom, calls=%fused_computation.50 | custom fusion | flops 2048 | bytes 772 | tf_op jit(solution)/shard_map/scatter-add | solution.py:80
  59.7 42.1 %all-reduce.4 = f32[64]{0:T(128)S(1)} all-reduce(f32[64]{0:T(128)S(1)} %bitcast.31), channel_id=2, replica_groups=mesh['gz'=4,'xy'=8] {'gz','xy'}, use_global_device_ids=true, to_apply=%region_4.5.clone | all-reduce | flops 64 | bytes 512
  101.8 0.6 dynamic-slice
  102.4 0.2 maximum_subtract_fusion.6
  102.7 0.8 fusion.6
  (33 shorter events, 0.5 us)
Async XLA Ops:
  0.6 7.7 %copy-start.2 = (f32[3,14,16,128]{3,2,1,0:T(8,128)S(1)}, f32[3,14,16,128]{3,2,1,0:T(8,128)}, u32[]{:S(2)}) copy-start(f32[3,14,16,128]{3,2,1,0:T(8,128)} %param.8) | copy-start | bytes 1032196
  9.3 8.0 %collective-permute-start = (f32[3,1,16,128]{3,2,1,0:T(8,128)S(1)}, f32[3,1,16,128]{3,2,1,0:T(8,128)S(1)}, u32[]{:S(2)}, u32[]{:S(2)}) collective-permute-start(f32[3,1,16,128]{3,2,1,0:T(8,128)S(1)} %slice.228), channel_id=1, source_target_pairs={{8,0},{16,8},{24,16},{9,1},{17,9},{25,17},{10,2},{18,10},{26,18},{... | collective-permute-start | bytes 73736 | tf_op jit(solution)/shard_map/ppermute | solution.py:16
  10.7 6.6 %collective-permute-start.1 = (f32[3,14,1,128]{3,2,1,0:T(1,128)S(1)}, f32[3,14,1,128]{3,2,1,0:T(1,128)S(1)}, u32[]{:S(2)}, u32[]{:S(2)}) collective-permute-start(f32[3,14,1,128]{3,2,1,0:T(1,128)S(1)} %slice.232), channel_id=1, source_target_pairs={{1,0},{2,1},{3,2},{4,3},{5,4},{6,5},{7,6},{9,8},{10,9},{11,10},{12... | collective-permute-start | bytes 64520 | tf_op jit(solution)/shard_map/ppermute | solution.py:16
  17.4 1.0 copy-start.1
  18.5 8.4 %collective-permute-start.2 = (f32[3,1,16,128]{3,2,1,0:T(8,128)S(1)}, f32[3,1,16,128]{3,2,1,0:T(8,128)S(1)}, u32[]{:S(2)}, u32[]{:S(2)}) collective-permute-start(f32[3,1,16,128]{3,2,1,0:T(8,128)S(1)} %slice.238), channel_id=1, source_target_pairs={{0,8},{8,16},{16,24},{1,9},{9,17},{17,25},{2,10},{10,18},{18,26},{... | collective-permute-start | bytes 73736 | tf_op jit(solution)/shard_map/ppermute | solution.py:16
  20.7 6.2 %collective-permute-start.3 = (f32[3,14,1,128]{3,2,1,0:T(1,128)S(1)}, f32[3,14,1,128]{3,2,1,0:T(1,128)S(1)}, u32[]{:S(2)}, u32[]{:S(2)}) collective-permute-start(f32[3,14,1,128]{3,2,1,0:T(1,128)S(1)} %slice.242), channel_id=1, source_target_pairs={{0,1},{1,2},{2,3},{3,4},{4,5},{5,6},{6,7},{8,9},{9,10},{10,11},{11... | collective-permute-start | bytes 64520 | tf_op jit(solution)/shard_map/ppermute | solution.py:16
  27.1 0.9 copy-start.3
  27.1 1.1 %copy-start.4 = (bf16[3,3,14,16,128]{4,3,2,1,0:T(8,128)(2,1)S(1)}, bf16[3,3,14,16,128]{4,3,2,1,0:T(8,128)(2,1)}, u32[]{:S(2)}) copy-start(bf16[3,3,14,16,128]{4,3,2,1,0:T(8,128)(2,1)} %param.11) | copy-start | bytes 1548292
  28.4 2.7 %copy-start.5 = (s32[14,16,128]{2,1,0:T(8,128)S(1)}, s32[14,16,128]{2,1,0:T(8,128)}, u32[]{:S(2)}) copy-start(s32[14,16,128]{2,1,0:T(8,128)} %param.13) | copy-start | bytes 344068
  28.5 8.0 %collective-permute-start.5 = (f32[3,14,1,128]{3,2,1,0:T(1,128)S(1)}, f32[3,14,1,128]{3,2,1,0:T(1,128)S(1)}, u32[]{:S(2)}, u32[]{:S(2)}) collective-permute-start(f32[3,14,1,128]{3,2,1,0:T(1,128)S(1)} %slice.254), channel_id=1, source_target_pairs={{1,0},{2,1},{3,2},{4,3},{5,4},{6,5},{7,6},{9,8},{10,9},{11,10},{12... | collective-permute-start | bytes 64520 | tf_op jit(solution)/shard_map/ppermute | solution.py:16
  29.8 6.7 %collective-permute-start.4 = (f32[3,1,16,128]{3,2,1,0:T(8,128)S(1)}, f32[3,1,16,128]{3,2,1,0:T(8,128)S(1)}, u32[]{:S(2)}, u32[]{:S(2)}) collective-permute-start(f32[3,1,16,128]{3,2,1,0:T(8,128)S(1)} %slice.250), channel_id=1, source_target_pairs={{8,0},{16,8},{24,16},{9,1},{17,9},{25,17},{10,2},{18,10},{26,18},{... | collective-permute-start | bytes 73736 | tf_op jit(solution)/shard_map/ppermute | solution.py:16
  36.8 65.6 %copy-start = (f32[3,14,16,128]{3,2,1,0:T(8,128)}, f32[3,14,16,128]{3,2,1,0:T(8,128)S(1)}, u32[]{:S(2)}) copy-start(f32[3,14,16,128]{3,2,1,0:T(8,128)S(1)} %maximum_add_fusion.1) | copy-start | bytes 1032196
  36.8 65.6 %collective-permute-start.7 = (f32[3,14,1,128]{3,2,1,0:T(1,128)S(1)}, f32[3,14,1,128]{3,2,1,0:T(1,128)S(1)}, u32[]{:S(2)}, u32[]{:S(2)}) collective-permute-start(f32[3,14,1,128]{3,2,1,0:T(1,128)S(1)} %slice.264), channel_id=1, source_target_pairs={{0,1},{1,2},{2,3},{3,4},{4,5},{5,6},{6,7},{8,9},{9,10},{10,11},{11... | collective-permute-start | bytes 64520 | tf_op jit(solution)/shard_map/ppermute | solution.py:16
  41.7 60.7 %collective-permute-start.6 = (f32[3,1,16,128]{3,2,1,0:T(8,128)S(1)}, f32[3,1,16,128]{3,2,1,0:T(8,128)S(1)}, u32[]{:S(2)}, u32[]{:S(2)}) collective-permute-start(f32[3,1,16,128]{3,2,1,0:T(8,128)S(1)} %slice.260), channel_id=1, source_target_pairs={{0,8},{8,16},{16,24},{1,9},{9,17},{17,25},{2,10},{10,18},{18,26},{... | collective-permute-start | bytes 73736 | tf_op jit(solution)/shard_map/ppermute | solution.py:16
where the time goes:
time: 104 us; the launch traced here: 103 us
  blocking collectives  42.1 us (40%)
  other arithmetic  29 us (28%)
  starting transfers between devices  20.1 us (19%)
  waiting for transfers between devices  6.57 us (6%)
  local copies, waits for them, and re-layouts  4.72 us (5%)
    unnamed x1, blocking collectives  42.1 us
    ppermute x8, starting transfers between devices, shifted(): lax.ppermute(value, axis, [(source, source + steps) for source in range(l...  20.1 us
    scatter-add x1, other arithmetic, on_device(): jax.ops.segment_sum(columns.reshape(-1), block_map.reshape(-1), num_segme...  14.8 us
    ppermute x8, waiting for transfers between devices, shifted(): lax.ppermute(value, axis, [(source, source + steps) for source in range(l...  6.57 us
    div x1, other arithmetic, on_device(): decay = (1.0 - sigma) / (1.0 + sigma)  6.1 us
    reduce_sum x1, other arithmetic, on_device(): columns = jnp.sum(cell_grad, 0) / (cell_grad.shape[0] * lax.axis_size('gz'))  5.14 us
    unnamed x13, local copies, waits for them, and re-layouts  2.58 us
  transfers between devices with their start and end apart: 8, of which 2 were waited for; matrix products, arithmetic and copies ran while one was open for 20% of the time, Pallas kernels for 0%

commit v1 on v0

v1 whole, which is shorter than its diff:
```python
import functools

import jax
import jax.numpy as jnp
from jax import lax
from jax.experimental import pallas as pl
from jax.experimental.pallas import tpu as pltpu
from jax.sharding import PartitionSpec as P

B_DEV = 2

DT_STEP = 0.5
SIGMA_UNIT = 0.15

V0, V1, V2, Q0, Q1, Q2, DR, H0, H1, H2 = range(10)
DECAY, INV = 7, 8
ALL = tuple(range(10))

Z_TOP = [(c, -1) for c in ALL] + [(c, -2) for c in (V0, V1, V2, H0, H1)]
Z_BOT = [(c, 0) for c in (V0, V1, V2, Q0, Q1, DR, H0, H1, H2)] + [(V0, 1), (V1, 1)]
X_TOP = [(c, -1) for c in ALL] + [(c, -2) for c in (V0, V1, V2, H1, H2)]
X_BOT = [(c, 0) for c in (V0, V1, V2, Q1, Q2, DR, H0, H1, H2)] + [(V1, 1), (V2, 1)]
SLOTS = len(Z_TOP)

VMEM = pl.BlockSpec(memory_space=pltpu.VMEM)
SMEM = pl.BlockSpec(memory_space=pltpu.SMEM)
ANY = pl.BlockSpec(memory_space=pl.ANY)


def round_up(value, unit):
    return -(-value // unit) * unit


def prepare_kernel(nz, nx, eps, e, h, s, mat, pml, vqd, za, zb, xa, xb):
    cells = nz * nx
    inverse = [1.0 / jnp.full((nx, 128), eps[k], jnp.float32) for k in range(eps.shape[0])]
    for z in range(nz):
        rows = pl.ds(z * nx, nx)
        kind = mat[rows, :]
        inv = inverse[0]
        for k in range(1, len(inverse)):
            inv = jnp.where(kind == k, inverse[k], inv)
        sigma = SIGMA_UNIT * pml[rows, :].astype(jnp.float32)
        recip = 1.0 / (1.0 + sigma)
        decay = (1.0 - sigma) * recip
        drive = DT_STEP * inv * recip
        vqd[pl.ds(DR * cells + z * nx, nx), :] = drive
        vqd[pl.ds(DECAY * cells + z * nx, nx), :] = decay
        vqd[pl.ds(INV * cells + z * nx, nx), :] = inv
        for c in range(3):
            at = pl.ds(c * cells + z * nx, nx)
            source = s[at, :].astype(jnp.float32)
            incoming = e[at, :] + source
            vqd[at, :] = drive * incoming
            vqd[pl.ds((Q0 + c) * cells + z * nx, nx), :] = decay * incoming + source

    def layer(c, z):
        if c < H0:
            return vqd[pl.ds(c * cells + z * nx, nx), :]
        return h[pl.ds((c - H0) * cells + z * nx, nx), :]

    def column(c, x):
        if c < H0:
            return vqd[pl.ds(c * cells + x, nz, stride=nx), :]
        return h[pl.ds((c - H0) * cells + x, nz, stride=nx), :]

    def pack_z(top, bottom):
        for slot, (c, dz) in enumerate(Z_TOP):
            top[pl.ds(slot * nx, nx), :] = layer(c, nz + dz)
        for slot, (c, dz) in enumerate(Z_BOT):
            bottom[pl.ds(slot * nx, nx), :] = layer(c, dz)

    def pack_x(top, bottom):
        for slot, (c, dx) in enumerate(X_TOP):
            top[pl.ds(slot * nz, nz), :] = column(c, nx + dx)
        for slot, (c, dx) in enumerate(X_BOT):
            bottom[pl.ds(slot * nz, nz), :] = column(c, dx)

    odd_z = lax.rem(lax.axis_index("gz"), 2) == 1
    odd_x = lax.rem(lax.axis_index("xy"), 2) == 1
    for odd, pack, first, second in ((odd_z, pack_z, za, zb), (odd_x, pack_x, xa, xb)):
        pl.when(jnp.logical_not(odd))(functools.partial(pack, first, second))
        pl.when(odd)(functools.partial(pack, second, first))


def corner_kernel(nz, nx, za, zb, xa_in, xb_in, xa, xb, top, bottom, sems):
    base = round_up(SLOTS * nz, 8)

    def gather(low, high):
        for slots, out in ((X_TOP, top), (X_BOT, bottom)):
            for slot, (c, dx) in enumerate(slots):
                x = dx if dx >= 0 else nx + dx
                for k, (ref, sent, dz) in enumerate(
                    ((low, Z_TOP, -2), (low, Z_TOP, -1), (high, Z_BOT, 0), (high, Z_BOT, 1))
                ):
                    if (c, dz) in sent:
                        row = sent.index((c, dz)) * nx + x
                        out[pl.ds(slot * 4 + k, 1), :] = ref[pl.ds(row, 1), :]

    odd_z = lax.rem(lax.axis_index("gz"), 2) == 1
    odd_x = lax.rem(lax.axis_index("xy"), 2) == 1
    pl.when(jnp.logical_not(odd_z))(functools.partial(gather, zb, za))
    pl.when(odd_z)(functools.partial(gather, za, zb))

    def put(first, second):
        window = pl.ds(base, top.shape[0])
        one = pltpu.make_async_copy(first, xa.at[window, :], sems.at[0])
        two = pltpu.make_async_copy(second, xb.at[window, :], sems.at[1])
        one.start()
        two.start()
        one.wait()
        two.wait()

    pl.when(jnp.logical_not(odd_x))(functools.partial(put, top, bottom))
    pl.when(odd_x)(functools.partial(put, bottom, top))


def weight_kernel(nz, nx, e, s, saved, vqd, weight, column):
    cells = nz * nx
    total = jnp.zeros((nx, 128), jnp.float32)
    for z in range(nz):
        decay = vqd[pl.ds(DECAY * cells + z * nx, nx), :]
        inv = vqd[pl.ds(INV * cells + z * nx, nx), :]
        cell = jnp.zeros((nx, 128), jnp.float32)
        for c in range(3):
            at = pl.ds(c * cells + z * nx, nx)
            times = [
                saved[pl.ds((3 * t + c) * cells + z * nx, nx), :].astype(jnp.float32)
                for t in range(3)
            ]
            incoming = e[at, :] + s[at, :].astype(jnp.float32)
            cell = cell + incoming * (times[2] - decay * times[1])
            weight[at, :] = (times[1] - decay * times[0]) * inv
        total = total + cell * inv
    column[...] = total


def march_kernel(
    nz, nx, layers, vqd, h, weight, column, za, zb, xa, xb, blocks, out_e, out_h, sums, zh, xh
):
    cells = nz * nx
    base = round_up(SLOTS * nz, 8)
    deep = nz + 4
    index_z, index_x = lax.axis_index("gz"), lax.axis_index("xy")
    odd_z, odd_x = lax.rem(index_z, 2) == 1, lax.rem(index_x, 2) == 1

    def take_z(low, high):
        zh[pl.ds(0, SLOTS * nx), :] = low[...]
        zh[pl.ds(SLOTS * nx, len(Z_BOT) * nx), :] = high[pl.ds(0, len(Z_BOT) * nx), :]

    def take_x(low, high):
        for slots, ref in ((X_TOP, low), (X_BOT, high)):
            for slot, (c, dx) in enumerate(slots):
                place = c * deep * 8 + dx % 8
                xh[pl.ds(place + 16, nz, stride=8), :] = ref[pl.ds(slot * nz, nz), :]
                xh[pl.ds(place, 2, stride=8), :] = ref[pl.ds(base + slot * 4, 2), :]
                upper = ref[pl.ds(base + slot * 4 + 2, 2), :]
                xh[pl.ds(place + (nz + 2) * 8, 2, stride=8), :] = upper

    pl.when(jnp.logical_not(odd_z))(functools.partial(take_z, zb, za))
    pl.when(odd_z)(functools.partial(take_z, za, zb))
    pl.when(jnp.logical_not(odd_x))(functools.partial(take_x, xb, xa))
    pl.when(odd_x)(functools.partial(take_x, xa, xb))

    tall = nx + 8
    lane = lax.broadcasted_iota(jnp.int32, (tall, 128), 1)
    row = lax.broadcasted_iota(jnp.int32, (tall, 128), 0)
    last, first = lane == 127, lane == 0
    inside_x = jnp.logical_or(row < nx + 4, jnp.broadcast_to(index_x, (tall, 128)) > 0)
    inside_z = jnp.logical_and(inside_x, jnp.broadcast_to(index_z, (tall, 128)) > 0)

    def load(c, z):
        side = xh[pl.ds((c * deep + z + 2) * 8, 8), :]
        if z < 0:
            own = zh[pl.ds(Z_TOP.index((c, z)) * nx, nx), :]
        elif z >= nz:
            own = zh[pl.ds((SLOTS + Z_BOT.index((c, z - nz))) * nx, nx), :]
        elif c < H0:
            own = vqd[pl.ds(c * cells + z * nx, nx), :]
        else:
            own = h[pl.ds((c - H0) * cells + z * nx, nx), :]
        return jnp.concatenate([own, side], axis=0)

    def next_y(f):
        return jnp.where(last, 0.0, pltpu.roll(f, 127, 1)) - f

    def prev_y(f):
        return f - jnp.where(first, 0.0, pltpu.roll(f, 1, 1))

    def next_x(f):
        return pltpu.roll(f, tall - 1, 0) - f

    def prev_x(f):
        return f - pltpu.roll(f, 1, 0)

    def magnetic(z, old, here, above, want_z):
        keep = inside_z if z < 0 else inside_x
        out = [
            old[0] + (next_y(here[2]) - (above[1] - here[1])),
            old[1] + ((above[0] - here[0]) - next_x(here[2])),
        ]
        if want_z:
            out.append(old[2] + (next_x(here[1]) - next_y(here[0])))
        return [jnp.where(keep, f, 0.0) for f in out]

    def curl_p(here, below, want_z):
        out = [
            prev_y(here[2]) - (here[1] - below[1]),
            (here[0] - below[0]) - prev_x(here[2]),
        ]
        if want_z:
            out.append(prev_x(here[1]) - prev_y(here[0]))
        return out

    total = column[...]
    v_here = [load(c, -2) for c in (V0, V1, V2)]
    mag_below, mag2_below = None, None
    inc_below, drv_below, mag_mid = None, None, None
    for z in range(-2, nz + 1):
        v_above = [load(c, z + 1) for c in ((V0, V1, V2) if z < nz else (V0, V1))]
        comps = (H0, H1) if z == -2 else (H0, H1, H2)
        mag = magnetic(z, [load(c, z) for c in comps], v_here, v_above, z > -2)
        v_here = v_above
        if z > -2:
            full = z < nz
            curl = curl_p(mag, mag_below, full)
            inc = [load(Q0 + c, z) - DT_STEP * curl[c] for c in range(3 if full else 2)]
            drive = load(DR, z)
            drv = [drive * f for f in inc]
            if 0 <= z < nz:
                cell = jnp.zeros((nx, 128), jnp.float32)
                for c in range(3):
                    cell = cell + inc[c][:nx] * weight[pl.ds(c * cells + z * nx, nx), :]
                total = total + cell
            if z > -1:
                low = z - 1
                mag2 = magnetic(low, mag_mid, drv_below, drv, low >= 0)
                if low >= 0:
                    decay = vqd[pl.ds(DECAY * cells + low * nx, nx), :]
                    curl = curl_p(mag2, mag2_below, True)
                    for c in range(3):
                        at = pl.ds(c * cells + low * nx, nx)
                        out_h[at, :] = mag2[c][:nx]
                        out_e[at, :] = decay * inc_below[c][:nx] - DT_STEP * curl[c][:nx]
                mag2_below = mag2
            inc_below, drv_below = inc, drv
        mag_mid, mag_below = mag, mag

    devices = sums.shape[0]
    total = total * (-1.0 / layers)
    owner = B_DEV * lax.broadcasted_iota(jnp.int32, (devices, 128), 0)
    spot = lax.broadcasted_iota(jnp.int32, (devices, 128), 1)
    parts = [jnp.zeros((devices, 128), jnp.float32) for _ in range(B_DEV)]
    for group in range(nx // 4):
        four = jnp.sum(total[4 * group : 4 * group + 4], axis=0, keepdims=True)
        label = blocks[pl.ds(4 * group, 1), :]
        for k in range(B_DEV):
            parts[k] = parts[k] + jnp.where(label == owner + k, four, 0.0)
    packed = jnp.zeros((devices, 128), jnp.float32)
    for k in range(B_DEV):
        packed = jnp.where(spot == k, jnp.sum(parts[k], axis=1, keepdims=True), packed)
    sums[...] = packed


def swap_pairs(count, offset):
    pairs = []
    for low in range(offset, count - 1, 2):
        pairs += [(low, low + 1), (low + 1, low)]
    return pairs


def estimate(flops, moved):
    return pl.CostEstimate(flops=flops, bytes_accessed=moved, transcendentals=0)


def on_device(
    adjoint_e, adjoint_h, source_e, e_saved, material_eps, material_id, pml_level, block_map
):
    nz, nx, ny = material_id.shape
    slabs, tiles = lax.axis_size("gz"), lax.axis_size("xy")
    cells = nz * nx
    f32 = jnp.float32
    flat = lambda a: a.reshape(-1, ny)
    e, h, s, saved = flat(adjoint_e), flat(adjoint_h), flat(source_e), flat(e_saved)
    mat, pml = flat(material_id), flat(pml_level)
    base = round_up(SLOTS * nz, 8)
    corner = round_up(SLOTS * 4, 8)
    z_msg = jax.ShapeDtypeStruct((SLOTS * nx, ny), f32)
    x_msg = jax.ShapeDtypeStruct((base + corner, ny), f32)
    params = pltpu.CompilerParams(vmem_limit_bytes=24 * 1024 * 1024)

    vqd, za, zb, xa, xb = pl.pallas_call(
        functools.partial(prepare_kernel, nz, nx),
        out_shape=(jax.ShapeDtypeStruct((9 * cells, ny), f32), z_msg, z_msg, x_msg, x_msg),
        in_specs=[SMEM] + [VMEM] * 5,
        out_specs=(VMEM,) * 5,
        compiler_params=params,
        cost_estimate=estimate(60 * cells * ny, 4 * 20 * cells * ny),
        name="prepare",
    )(material_eps, e, h, s, mat, pml)

    za = lax.ppermute(za, "gz", swap_pairs(slabs, 0))
    zb = lax.ppermute(zb, "gz", swap_pairs(slabs, 1))

    weight, column = pl.pallas_call(
        functools.partial(weight_kernel, nz, nx),
        out_shape=(
            jax.ShapeDtypeStruct((3 * cells, ny), f32),
            jax.ShapeDtypeStruct((nx, ny), f32),
        ),
        in_specs=[VMEM] * 4,
        out_specs=(VMEM,) * 2,
        compiler_params=params,
        cost_estimate=estimate(40 * cells * ny, 4 * 16 * cells * ny),
        name="weights",
    )(e, s, saved, vqd)

    xa, xb = pl.pallas_call(
        functools.partial(corner_kernel, nz, nx),
        out_shape=(x_msg, x_msg),
        in_specs=[VMEM, VMEM, ANY, ANY],
        out_specs=(ANY, ANY),
        scratch_shapes=[
            pltpu.VMEM((corner, ny), f32),
            pltpu.VMEM((corner, ny), f32),
            pltpu.SemaphoreType.DMA((2,)),
        ],
        input_output_aliases={2: 0, 3: 1},
        compiler_params=params,
        cost_estimate=estimate(cells * ny, 4 * cells * ny),
        name="corners",
    )(za, zb, xa, xb)

    xa = lax.ppermute(xa, "xy", swap_pairs(tiles, 0))
    xb = lax.ppermute(xb, "xy", swap_pairs(tiles, 1))

    field_e, field_h, sums = pl.pallas_call(
        functools.partial(march_kernel, nz, nx, nz * slabs),
        out_shape=(
            jax.ShapeDtypeStruct((3 * cells, ny), f32),
            jax.ShapeDtypeStruct((3 * cells, ny), f32),
            jax.ShapeDtypeStruct((slabs * tiles, ny), f32),
        ),
        in_specs=[VMEM] * 9,
        out_specs=(VMEM,) * 3,
        scratch_shapes=[
            pltpu.VMEM(((SLOTS + len(Z_BOT)) * nx, ny), f32),
            pltpu.VMEM((10 * (nz + 4) * 8, ny), f32),
        ],
        compiler_params=params,
        cost_estimate=estimate(200 * cells * ny, 4 * 30 * cells * ny),
        name="march",
    )(vqd, h, weight, column, za, zb, xa, xb, block_map)

    gathered = lax.all_to_all(sums, ("gz", "xy"), 0, 0, tiled=True)
    design_grad = jnp.sum(gathered, axis=0)[:B_DEV]
    return field_e.reshape(adjoint_e.shape), field_h.reshape(adjoint_h.shape), design_grad


def solution(mesh):
    placed = (
        P(None, "gz", "xy", None),
        P(None, "gz", "xy", None),
        P(None, "gz", "xy", None),
        P(None, None, "gz", "xy", None),
        P(),
        P("gz", "xy", None),
        P("gz", "xy", None),
        P("xy", None),
    )
    return jax.shard_map(
        on_device,
        mesh=mesh,
        in_specs=placed,
        out_specs=(P(None, "gz", "xy", None), P(None, "gz", "xy", None), P(("gz", "xy"))),
        check_vma=False,
    )
```

time: 104 us -> 38.8 us (0.37)
  other arithmetic: 29 us -> 0.56 us
  blocking collectives: 42.1 us -> 21.6 us
  starting transfers between devices: 20.1 us -> 4.77 us
  waiting for transfers between devices: 6.57 us -> 2.52 us
  Pallas kernels: 0 us -> 2.95 us
    unnamed x1 -> x0, blocking collectives: 42.1 us -> none
    all_to_all x0 -> x1, blocking collectives: none -> 21.6 us  [on_device(): gathered = lax.all_to_all(sums, ('gz', 'xy'), 0, 0, tiled=True)]
    ppermute x8 -> x4, starting transfers between devices: 20.1 us -> 4.77 us  [the longest x1 2.94 us: on_device(): xa = lax.ppermute(xa, 'xy', swap_pairs(tiles, 0))]
    scatter-add x1 -> x0, other arithmetic: 14.8 us -> none  [on_device(): jax.ops.segment_sum(columns.reshape(-1), block_map.reshape(-1), num_segme...]
    div x2 -> x0, other arithmetic: 6.1 us -> none  [the longest x1 6.1 us: on_device(): decay = (1.0 - sigma) / (1.0 + sigma)]
    reduce_sum x2 -> x1, other arithmetic: 5.34 us -> 0.56 us  [on_device(): design_grad = jnp.sum(gathered, axis=0)[:B_DEV]]
    ppermute x8 -> x4, waiting for transfers between devices: 6.57 us -> 2.52 us  [the longest x1 2.21 us: on_device(): xa = lax.ppermute(xa, 'xy', swap_pairs(tiles, 0))]
    pallas_call x0 -> x4, Pallas kernels: none -> 2.95 us  [the longest x1 1.87 us: on_device(): pl.pallas_call(functools.partial(march_kernel, nz, nx, nz * slabs), out_s...]
  transfers between devices with their start and end apart: 8 -> 4, of which waited for: 2 -> 2; matrix products, arithmetic and copies ran while one was open for 20% -> 0% of each run, Pallas kernels for 0% -> 0%
where the time goes in v1:
time: 38.8 us; the launch traced here: 38.5 us
  blocking collectives  21.6 us (56%)
  local copies, waits for them, and re-layouts  5.34 us (14%)
  starting transfers between devices  4.77 us (12%)
  Pallas kernels  2.95 us (8%)
  waiting for transfers between devices  2.52 us (6%)
  between operations  0.73 us (2%)
  other arithmetic  0.56 us (1%)
    all_to_all x1, blocking collectives, on_device(): gathered = lax.all_to_all(sums, ('gz', 'xy'), 0, 0, tiled=True)  21.6 us
    unnamed x22, local copies, waits for them, and re-layouts  5.34 us
    ppermute x1, starting transfers between devices, on_device(): xa = lax.ppermute(xa, 'xy', swap_pairs(tiles, 0))  2.94 us
    ppermute x1, waiting for transfers between devices, on_device(): xa = lax.ppermute(xa, 'xy', swap_pairs(tiles, 0))  2.21 us
    pallas_call x1, Pallas kernels, on_device(): pl.pallas_call(functools.partial(march_kernel, nz, nx, nz * slabs), out_s...  1.87 us
    pallas_call x1, Pallas kernels, on_device(): pl.pallas_call(functools.partial(prepare_kernel, nz, nx), out_shape=(jax....  0.79 us
  transfers between devices with their start and end apart: 4, of which 2 were waited for; matrix products, arithmetic and copies ran while one was open for 0% of the time, Pallas kernels for 0%

profile of v1, /device:TPU:0, one launch (start us, length us, event | category | flops | bytes accessed | tf_op | source)
XLA Modules:
  0.0 38.5 jit_solution(9636699811085509119)
XLA Ops:
  0.6 0.0 copy-start.10
  0.6 0.6 %copy-done.10 = f32[8]{0:T(128)S(1)} copy-done((f32[8]{0:T(128)S(1)}, f32[8]{0:T(128)}, u32[]{:S(2)}) %copy-start.10) | copy-done | bytes 56
  1.3 0.0 copy-start
  1.3 1.0 %copy-done = f32[3,14,16,128]{3,2,1,0:T(8,128)S(1)} copy-done((f32[3,14,16,128]{3,2,1,0:T(8,128)S(1)}, f32[3,14,16,128]{3,2,1,0:T(8,128)}, u32[]{:S(2)}) %copy-start) | copy-done | bytes 344088
  2.3 0.0 copy-start.2
  2.3 1.0 %copy-done.2 = f32[3,14,16,128]{3,2,1,0:T(8,128)S(1)} copy-done((f32[3,14,16,128]{3,2,1,0:T(8,128)S(1)}, f32[3,14,16,128]{3,2,1,0:T(8,128)}, u32[]{:S(2)}) %copy-start.2) | copy-done | bytes 344088
  3.2 0.0 copy-start.4
  3.2 0.9 %copy-done.4 = bf16[3,14,16,128]{3,2,1,0:T(8,128)(2,1)S(1)} copy-done((bf16[3,14,16,128]{3,2,1,0:T(8,128)(2,1)S(1)}, bf16[3,14,16,128]{3,2,1,0:T(8,128)(2,1)}, u32[]{:S(2)}) %copy-start.4) | copy-done | bytes 172056
  4.2 0.9 %copy-done.7 = s32[14,16,128]{2,1,0:T(8,128)S(1)} copy-done((s32[14,16,128]{2,1,0:T(8,128)S(1)}, s32[14,16,128]{2,1,0:T(8,128)}, u32[]{:S(2)}) %copy-start.7) | copy-done | bytes 114712
  5.1 0.9 %copy-done.8 = s32[14,16,128]{2,1,0:T(8,128)S(1)} copy-done((s32[14,16,128]{2,1,0:T(8,128)S(1)}, s32[14,16,128]{2,1,0:T(8,128)}, u32[]{:S(2)}) %copy-start.8) | copy-done | bytes 114712
  6.0 0.8 %prepare.1 = (f32[2016,128]{1,0:T(8,128)S(1)}, f32[240,128]{1,0:T(8,128)S(1)}, f32[240,128]{1,0:T(8,128)S(1)}, f32[280,128]{1,0:T(8,128)S(1)}, f32[280,128]{1,0:T(8,128)S(1)}) custom-call(f32[8]{0:T(128)S(1)} %copy-done.10, f32[672,128]{1,0:T(8,128)S(1)} %bitcast.14, f32[672,128]{1,0:T(8,128)S(1)} %bitcast.12, bf16[672,128]{1,0:T(8,128)(2,1)S(1)} %bitcast.16, ...), custom_call_target="tpu_custom_call" | custom-call | flops 1720320 | bytes 2293760 | tf_op jit(solution)/shard_map/prepare/pallas_call | solution.py:292
  6.8 0.0 copy-start.3
  6.8 0.5 %collective-permute-start = (f32[240,128]{1,0:T(8,128)S(1)}, f32[240,128]{1,0:T(8,128)S(1)}, u32[]{:S(2)}, u32[]{:S(2)}) collective-permute-start(f32[240,128]{1,0:T(8,128)S(1)} %get-tuple-element.18), channel_id=1, source_target_pairs={{0,8},{8,0},{16,24},{24,16},{1,9},{9,1},{17,25},{25,17},{2,10},{10... | collective-permute-start | bytes 368648 | tf_op jit(solution)/shard_map/ppermute | solution.py:302
  7.3 0.7 %collective-permute-start.1 = (f32[240,128]{1,0:T(8,128)S(1)}, f32[240,128]{1,0:T(8,128)S(1)}, u32[]{:S(2)}, u32[]{:S(2)}) collective-permute-start(f32[240,128]{1,0:T(8,128)S(1)} %get-tuple-element.19), channel_id=1, source_target_pairs={{8,16},{16,8},{9,17},{17,9},{10,18},{18,10},{11,19},{19,11},{12,20... | collective-permute-start | bytes 368648 | tf_op jit(solution)/shard_map/ppermute | solution.py:303
  8.0 0.3 collective-permute-done.za
  8.3 0.0 collective-permute-done.1.zb
  8.3 0.1 corners.1
  8.4 2.9 %collective-permute-start.2 = (f32[280,128]{1,0:T(8,128)S(1)}, f32[280,128]{1,0:T(8,128)S(1)}, u32[]{:S(2)}, u32[]{:S(2)}) collective-permute-start(f32[280,128]{1,0:T(8,128)S(1)} %get-tuple-element.22), channel_id=1, source_target_pairs={{0,1},{1,0},{2,3},{3,2},{4,5},{5,4},{6,7},{7,6},{8,9},{9,8},{10,11... | collective-permute-start | bytes 430088 | tf_op jit(solution)/shard_map/ppermute | solution.py:334
  11.4 0.7 %collective-permute-start.3 = (f32[280,128]{1,0:T(8,128)S(1)}, f32[280,128]{1,0:T(8,128)S(1)}, u32[]{:S(2)}, u32[]{:S(2)}) collective-permute-start(f32[280,128]{1,0:T(8,128)S(1)} %get-tuple-element.23), channel_id=1, source_target_pairs={{1,2},{2,1},{3,4},{4,3},{5,6},{6,5},{9,10},{10,9},{11,12},{12,11},... | collective-permute-start | bytes 430088 | tf_op jit(solution)/shard_map/ppermute | solution.py:335
  12.0 0.0 copy-done.6
  12.0 0.0 copy-done.3
  12.0 0.0 copy-done.5
  12.1 0.0 copy-start.1
  12.1 0.0 copy-start.9
  12.1 0.2 weights.1
  12.2 2.2 %collective-permute-done.2.xa = f32[280,128]{1,0:T(8,128)S(1)} collective-permute-done((f32[280,128]{1,0:T(8,128)S(1)}, f32[280,128]{1,0:T(8,128)S(1)}, u32[]{:S(2)}, u32[]{:S(2)}) %collective-permute-start.2) | collective-permute-done | bytes 143392 | tf_op jit(solution)/shard_map/ppermute | solution.py:334
  14.4 0.0 collective-permute-done.3.xb
  14.4 0.0 copy-done.1
  14.4 0.0 copy-done.9
  14.5 1.9 %march.1 = (f32[672,128]{1,0:T(8,128)}, f32[672,128]{1,0:T(8,128)}, f32[32,128]{1,0:T(8,128)S(1)}) custom-call(f32[2016,128]{1,0:T(8,128)S(1)} %get-tuple-element.15.vqd, f32[672,128]{1,0:T(8,128)S(1)} %bitcast.13, f32[672,128]{1,0:T(8,128)S(1)} %get-tuple-element.16.weight, f32[16,128]{1,0:T(8,128)S(1)} %get-tuple-element.17.column, ...), custom_call_target="tpu_custom_call" | custom-call | flops 5734400 | bytes 3440640 | tf_op jit(solution)/shard_map/march/pallas_call | solution.py:337
  16.3 21.6 %all_to_all.9 = f32[32,1,128]{2,1,0:T(1,128)S(1)} all-to-all(f32[32,1,128]{2,1,0:T(1,128)S(1)} %bitcast.21), channel_id=1, replica_groups=mesh['gz'=4,'xy'=8] {'gz','xy'}, dimensions={0} | all-to-all | bytes 32768 | tf_op jit(solution)/shard_map/all_to_all | solution.py:355
  37.9 0.6 %reduce_sum.9 = f32[128]{0:T(128)} reduce(f32[32,1,128]{2,1,0:T(1,128)S(1)} %all_to_all.9, f32[]{:T(128)} %constant.0.clone.1), dimensions={0,1}, to_apply=%region_0.0 | reduce | flops 3968 | bytes 16900 | tf_op jit(solution)/shard_map/reduce_sum | solution.py:356
  (4 shorter events, 0.0 us)
Async XLA Ops:
  0.6 0.7 %copy-start.10 = (f32[8]{0:T(128)S(1)}, f32[8]{0:T(128)}, u32[]{:S(2)}) copy-start(f32[8]{0:T(128)} %eps.1) | copy-start | bytes 100
  1.3 1.0 %copy-start = (f32[3,14,16,128]{3,2,1,0:T(8,128)S(1)}, f32[3,14,16,128]{3,2,1,0:T(8,128)}, u32[]{:S(2)}) copy-start(f32[3,14,16,128]{3,2,1,0:T(8,128)} %param.9) | copy-start | bytes 1032196
  2.3 1.0 %copy-start.2 = (f32[3,14,16,128]{3,2,1,0:T(8,128)S(1)}, f32[3,14,16,128]{3,2,1,0:T(8,128)}, u32[]{:S(2)}) copy-start(f32[3,14,16,128]{3,2,1,0:T(8,128)} %param.8) | copy-start | bytes 1032196
  3.2 0.9 %copy-start.4 = (bf16[3,14,16,128]{3,2,1,0:T(8,128)(2,1)S(1)}, bf16[3,14,16,128]{3,2,1,0:T(8,128)(2,1)}, u32[]{:S(2)}) copy-start(bf16[3,14,16,128]{3,2,1,0:T(8,128)(2,1)} %param.10) | copy-start | bytes 516100
  4.2 0.9 %copy-start.7 = (s32[14,16,128]{2,1,0:T(8,128)S(1)}, s32[14,16,128]{2,1,0:T(8,128)}, u32[]{:S(2)}) copy-start(s32[14,16,128]{2,1,0:T(8,128)} %param.13) | copy-start | bytes 344068
  5.1 0.9 %copy-start.8 = (s32[14,16,128]{2,1,0:T(8,128)S(1)}, s32[14,16,128]{2,1,0:T(8,128)}, u32[]{:S(2)}) copy-start(s32[14,16,128]{2,1,0:T(8,128)} %param.14) | copy-start | bytes 344068
  6.0 6.1 %copy-start.6 = (bf16[3,3,14,16,128]{4,3,2,1,0:T(8,128)(2,1)S(1)}, bf16[3,3,14,16,128]{4,3,2,1,0:T(8,128)(2,1)}, u32[]{:S(2)}) copy-start(bf16[3,3,14,16,128]{4,3,2,1,0:T(8,128)(2,1)} %param.11) | copy-start | bytes 1548292
  6.8 5.3 %copy-start.3 = (f32[3,14,16,128]{3,2,1,0:T(8,128)S(1)}, f32[3,14,16,128]{3,2,1,0:T(8,128)}, u32[]{:S(2)}) copy-start(f32[3,14,16,128]{3,2,1,0:T(8,128)} %param.8) | copy-start | bytes 1032196
  6.8 1.5 %collective-permute-start = (f32[240,128]{1,0:T(8,128)S(1)}, f32[240,128]{1,0:T(8,128)S(1)}, u32[]{:S(2)}, u32[]{:S(2)}) collective-permute-start(f32[240,128]{1,0:T(8,128)S(1)} %get-tuple-element.18), channel_id=1, source_target_pairs={{0,8},{8,0},{16,24},{24,16},{1,9},{9,1},{17,25},{25,17},{2,10},{10... | collective-permute-start | bytes 368648 | tf_op jit(solution)/shard_map/ppermute | solution.py:302
  7.3 1.0 %collective-permute-start.1 = (f32[240,128]{1,0:T(8,128)S(1)}, f32[240,128]{1,0:T(8,128)S(1)}, u32[]{:S(2)}, u32[]{:S(2)}) collective-permute-start(f32[240,128]{1,0:T(8,128)S(1)} %get-tuple-element.19), channel_id=1, source_target_pairs={{8,16},{16,8},{9,17},{17,9},{10,18},{18,10},{11,19},{19,11},{12,20... | collective-permute-start | bytes 368648 | tf_op jit(solution)/shard_map/ppermute | solution.py:303
  8.3 3.8 %copy-start.5 = (bf16[3,14,16,128]{3,2,1,0:T(8,128)(2,1)S(1)}, bf16[3,14,16,128]{3,2,1,0:T(8,128)(2,1)}, u32[]{:S(2)}) copy-start(bf16[3,14,16,128]{3,2,1,0:T(8,128)(2,1)} %param.10) | copy-start | bytes 516100
  8.4 6.0 %collective-permute-start.2 = (f32[280,128]{1,0:T(8,128)S(1)}, f32[280,128]{1,0:T(8,128)S(1)}, u32[]{:S(2)}, u32[]{:S(2)}) collective-permute-start(f32[280,128]{1,0:T(8,128)S(1)} %get-tuple-element.22), channel_id=1, source_target_pairs={{0,1},{1,0},{2,3},{3,2},{4,5},{5,4},{6,7},{7,6},{8,9},{9,8},{10,11... | collective-permute-start | bytes 430088 | tf_op jit(solution)/shard_map/ppermute | solution.py:334
  11.4 3.1 %collective-permute-start.3 = (f32[280,128]{1,0:T(8,128)S(1)}, f32[280,128]{1,0:T(8,128)S(1)}, u32[]{:S(2)}, u32[]{:S(2)}) collective-permute-start(f32[280,128]{1,0:T(8,128)S(1)} %get-tuple-element.23), channel_id=1, source_target_pairs={{1,2},{2,1},{3,4},{4,3},{5,6},{6,5},{9,10},{10,9},{11,12},{12,11},... | collective-permute-start | bytes 430088 | tf_op jit(solution)/shard_map/ppermute | solution.py:335
  12.1 2.4 %copy-start.1 = (f32[3,14,16,128]{3,2,1,0:T(8,128)S(1)}, f32[3,14,16,128]{3,2,1,0:T(8,128)}, u32[]{:S(2)}) copy-start(f32[3,14,16,128]{3,2,1,0:T(8,128)} %param.9) | copy-start | bytes 1032196
  12.1 2.4 %copy-start.9 = (s32[16,128]{1,0:T(8,128)S(1)}, s32[16,128]{1,0:T(8,128)}, u32[]{:S(2)}) copy-start(s32[16,128]{1,0:T(8,128)} %blocks.1) | copy-start | bytes 24580

commit v2 on v0

v2 whole, which is shorter than its diff:
```python
import functools

import jax
import jax.numpy as jnp
from jax import lax
from jax.experimental import pallas as pl
from jax.experimental.pallas import tpu as pltpu
from jax.sharding import PartitionSpec as P

B_DEV = 2

DT_STEP = 0.5
SIGMA_UNIT = 0.15

V0, V1, V2, Q0, Q1, Q2, DR, H0, H1, H2, I0, I1, I2, DECAY, INV = range(15)
FIELDS = 15

Z_LOW = (H0, H1, H2, Q0, Q1, Q2, DR)
Z_HIGH = (V0, V1, V2, Q0, Q1, DR, H1, H2)
X_LOW = (H1, H2, Q0, Q1, Q2, DR)
X_HIGH = (V1, V2, Q1, Q2, DR)
EXTRA_Z = 7
EXTRA_X = 5
Z_SLOTS, X_SLOTS = 8, 6

VMEM = pl.BlockSpec(memory_space=pltpu.VMEM)
HBM = pl.BlockSpec(memory_space=pltpu.HBM)


def shape_of(rows, ny):
    return jax.ShapeDtypeStruct((rows, ny), jnp.float32)


def is_odd(axis):
    return lax.rem(lax.axis_index(axis), 2) == 1


def either(odd, body, first, second):
    pl.when(jnp.logical_not(odd))(functools.partial(body, first, second))
    pl.when(odd)(functools.partial(body, second, first))


def masks(tall):
    row = lax.broadcasted_iota(jnp.int32, (tall, 128), 0)
    lane = lax.broadcasted_iota(jnp.int32, (tall, 128), 1)
    return row, lane == 0, lane == 127


def inverse_table(eps, nx):
    return [1.0 / jnp.full((nx, 128), eps[k], jnp.float32) for k in range(eps.shape[0])]


def cell_factors(kind, level, table):
    inv = table[0]
    for k in range(1, len(table)):
        inv = jnp.where(kind == k, table[k], inv)
    sigma = SIGMA_UNIT * level.astype(jnp.float32)
    recip = 1.0 / (1.0 + sigma)
    return (1.0 - sigma) * recip, DT_STEP * inv * recip, inv


def faces_kernel(nz, nx, eps_in, e_in, h_in, s_in, mat_in, pml_in, za, zb, eps, *rest):
    bufs, sems = rest[:-1], rest[-1]
    copies = [pltpu.make_async_copy(eps_in, eps, sems.at[0])]
    for k, ref in enumerate((e_in, h_in, s_in, mat_in, pml_in)):
        for side, start in enumerate((0, nz - 2)):
            part = pl.ds(start, 2)
            source = ref.at[:, part] if k < 3 else ref.at[part]
            copies.append(pltpu.make_async_copy(source, bufs[k].at[side], sems.at[len(copies)]))
    for copy in copies:
        copy.start()
    for copy in copies:
        copy.wait()
    e, h, s, mat, pml = bufs
    table = inverse_table(eps, nx)
    row, first, last = masks(nx)

    def next_y(f):
        return jnp.where(last, 0.0, pltpu.roll(f, 127, 1)) - f

    def next_x(f):
        return jnp.where(row == nx - 1, 0.0, pltpu.roll(f, nx - 1, 0)) - f

    def layer(side, z):
        decay, drive, _ = cell_factors(mat[side, z], pml[side, z], table)
        source = [s[side, c, z].astype(jnp.float32) for c in range(3)]
        incoming = [e[side, c, z] + source[c] for c in range(3)]
        v = [drive * f for f in incoming]
        q = [decay * f + g for f, g in zip(incoming, source)]
        return v, q, drive, [h[side, c, z] for c in range(3)]

    v, q, drive, mag = layer(1, 1)
    w, _, _, deep = layer(1, 0)
    deep_x = deep[0] + (next_y(w[2]) - (v[1] - w[1]))
    deep_y = deep[1] + ((v[0] - w[0]) - next_x(w[2]))
    low = [
        mag[0] + (next_y(v[2]) + v[1]),
        mag[1] - (v[0] + next_x(v[2])),
        mag[2] + (next_x(v[1]) - next_y(v[0])),
        q[0] - DT_STEP * deep_y,
        q[1] + DT_STEP * deep_x,
        q[2],
        drive,
        jnp.where(row == 0, v[1][:1], jnp.where(row == 1, v[2][:1], w[2][:1])),
    ]
    v, q, drive, mag = layer(0, 0)
    w, _, _, _ = layer(0, 1)
    edge_x = mag[0] + (next_y(v[2]) - (w[1] - v[1]))
    edge_y = mag[1] + (w[0] - v[0])
    high = [v[0], v[1], v[2], q[0], q[1] - DT_STEP * edge_x, drive, edge_y, mag[2]]

    def put(top, bottom):
        for slot in range(Z_SLOTS):
            top[pl.ds(slot * nx, nx), :] = low[slot]
            bottom[pl.ds(slot * nx, nx), :] = high[slot]

    either(is_odd("gz"), put, za, zb)


def prepare_kernel(nz, nx, eps_in, e_in, h_in, s_in, mat_in, pml_in, work, eps, *rest):
    bufs, sems = rest[:-1], rest[-1]
    copies = [
        pltpu.make_async_copy(source, target, sems.at[k])
        for k, (source, target) in enumerate(
            zip((eps_in, mat_in, pml_in, s_in, e_in, h_in), (eps,) + bufs)
        )
    ]
    for copy in copies:
        copy.start()
    mat, pml, s, e, h = bufs
    for copy in copies[:5]:
        copy.wait()
    table = inverse_table(eps, nx)
    tall = nx * (nz + 2)
    for z in range(nz):
        decay, drive, inv = cell_factors(mat[z], pml[z], table)

        def keep(field, value):
            work[pl.ds(field * tall + (z + 1) * nx, nx), :] = value

        keep(DR, drive)
        keep(DECAY, decay)
        keep(INV, inv)
        for c in range(3):
            source = s[c, z].astype(jnp.float32)
            incoming = e[c, z] + source
            keep(V0 + c, drive * incoming)
            keep(Q0 + c, decay * incoming + source)
            keep(I0 + c, incoming)
    copies[5].wait()
    for c in range(3):
        for z in range(nz):
            work[pl.ds((H0 + c) * tall + (z + 1) * nx, nx), :] = h[c, z]


def columns_kernel(nz, nx, za, zb, work, zh, xa, xb):
    tall = nx * (nz + 2)
    deep = nz + 2
    zero = jnp.zeros((nx, 128), jnp.float32)

    def take(low, high):
        for field in range(V0, H2 + 1):
            for k, (slots, ref) in enumerate(((Z_LOW, low), (Z_HIGH, high))):
                at = pl.ds((2 * field + k) * nx, nx)
                if field in slots:
                    zh[at, :] = ref[pl.ds(slots.index(field) * nx, nx), :]
                else:
                    zh[at, :] = zero

    odd_z = is_odd("gz")
    either(odd_z, take, zb, za)
    index = jnp.where(odd_z, 0, 1)
    row, first, last = masks(deep)

    def extra(k):
        at = pl.ds(EXTRA_Z * nx + k, 1)
        return jnp.where(jnp.broadcast_to(index, (1, 128)) == 0, za[at, :], zb[at, :])

    for k in range(2):
        zh[pl.ds(20 * nx + k, 1), :] = extra(k)

    def next_y(f):
        return jnp.where(last, 0.0, pltpu.roll(f, 127, 1)) - f

    def prev_y(f):
        return f - jnp.where(first, 0.0, pltpu.roll(f, 1, 1))

    def next_z(f):
        return jnp.where(row == deep - 1, 0.0, pltpu.roll(f, deep - 1, 0) - f)

    def prev_z(f):
        return f - jnp.where(row == 0, 0.0, pltpu.roll(f, 1, 0))

    def column(field, x):
        own = work[pl.ds(field * tall + x, deep, stride=nx), :]
        below, above = (zh[pl.ds((2 * field + k) * nx + x, 1), :] for k in range(2))
        return jnp.where(row == 0, below, jnp.where(row == deep - 1, above, own))

    bottom_edge = jnp.logical_and(row == 0, jnp.broadcast_to(lax.axis_index("gz"), row.shape) == 0)

    x = nx - 1
    v = [column(V0 + c, x) for c in range(3)]
    w = [column(V0 + c, x - 1) for c in range(3)]
    mag_x = column(H0, x) + (next_y(v[2]) - next_z(v[1]))
    mag_x = jnp.where(bottom_edge, 0.0, mag_x)
    deep_y = column(H1, x - 1) + (next_z(w[0]) - (v[2] - w[2]))
    deep_z = column(H2, x - 1) + ((v[1] - w[1]) - next_y(w[0]))
    low = [
        column(H1, x) + (next_z(v[0]) + v[2]),
        column(H2, x) - (v[1] + next_y(v[0])),
        column(Q0, x),
        column(Q1, x) - DT_STEP * (prev_z(mag_x) + deep_z),
        column(Q2, x) + DT_STEP * (deep_y + prev_y(mag_x)),
        column(DR, x),
    ]

    v = [column(V0 + c, 0) for c in range(3)]
    w = [column(V0 + c, 1) for c in range(3)]
    mag_x = column(H0, 0) + (next_y(v[2]) - next_z(v[1]))
    mag_x = jnp.where(bottom_edge, 0.0, mag_x)
    mag_y = column(H1, 0) + (next_z(v[0]) - (w[2] - v[2]))
    mag_z = column(H2, 0) + ((w[1] - v[1]) - next_y(v[0]))
    high = [
        jnp.where(row == 0, extra(0), v[1]),
        jnp.where(row == 0, extra(1), v[2]),
        column(Q1, 0) - DT_STEP * (prev_z(mag_x) - mag_z),
        column(Q2, 0) - DT_STEP * (mag_y - prev_y(mag_x)),
        column(DR, 0),
        jnp.broadcast_to(extra(2), (deep, 128)),
    ]

    def put(top, bottom):
        for slot in range(X_SLOTS):
            top[pl.ds(slot * deep, deep), :] = low[slot]
            bottom[pl.ds(slot * deep, deep), :] = high[slot]

    either(is_odd("xy"), put, xa, xb)


def weight_kernel(nz, nx, saved, work, weight, column):
    cells, tall = nz * nx, nx * (nz + 2)
    total = jnp.zeros((nx, 128), jnp.float32)
    for z in range(nz):
        near = pl.ds(DECAY * tall + (z + 1) * nx, nx)
        decay = work[near, :]
        inv = work[pl.ds(INV * tall + (z + 1) * nx, nx), :]
        cell = jnp.zeros((nx, 128), jnp.float32)
        for c in range(3):
            times = [
                saved[pl.ds((3 * t + c) * cells + z * nx, nx), :].astype(jnp.float32)
                for t in range(3)
            ]
            incoming = work[pl.ds((I0 + c) * tall + (z + 1) * nx, nx), :]
            cell = cell + incoming * (times[2] - decay * times[1])
            weight[pl.ds(c * cells + z * nx, nx), :] = (times[1] - decay * times[0]) * inv
        total = total + cell * inv
    column[...] = total


def march_kernel(
    nz, nx, layers, work, zh, weight, column, xa, xb, blocks, e_out, h_out, sums, xh, out_e, out_h, sems
):
    cells, tall, deep = nz * nx, nx * (nz + 2), nz + 2
    index_z, index_x = lax.axis_index("gz"), lax.axis_index("xy")
    odd_x = is_odd("xy")
    xh[...] = jnp.zeros_like(xh)

    def take(low, high):
        for slots, ref, place in ((X_LOW, low, 7), (X_HIGH, high, 0)):
            for slot, field in enumerate(slots):
                at = pl.ds(field * deep * 8 + place, deep, stride=8)
                xh[at, :] = ref[pl.ds(slot * deep, deep), :]

    either(odd_x, take, xb, xa)
    at = pl.ds(EXTRA_X * deep, 1)
    beyond = jnp.where(jnp.broadcast_to(odd_x, (1, 128)), xb[at, :], xa[at, :])

    rows = nx + 8
    row, first, last = masks(rows)
    inside_x = jnp.logical_or(
        row < nx, jnp.logical_and(row == rows - 1, jnp.broadcast_to(index_x, row.shape) > 0)
    )
    inside_z = jnp.logical_and(inside_x, jnp.broadcast_to(index_z, row.shape) > 0)

    def load(field, z):
        if 0 <= z < nz:
            own = work[pl.ds(field * tall + (z + 1) * nx, nx), :]
        else:
            own = zh[pl.ds((2 * field + (z > 0)) * nx, nx), :]
        side = xh[pl.ds((field * deep + z + 1) * 8, 8), :]
        return jnp.concatenate([own, side], axis=0)

    def next_y(f):
        return jnp.where(last, 0.0, pltpu.roll(f, 127, 1)) - f

    def prev_y(f):
        return f - jnp.where(first, 0.0, pltpu.roll(f, 1, 1))

    def next_x(f):
        return pltpu.roll(f, rows - 1, 0) - f

    def prev_x(f):
        return f - pltpu.roll(f, 1, 0)

    def magnetic(z, old, here, above):
        keep = inside_z if z < 0 else inside_x
        out = [
            old[0] + (next_y(here[2]) - (above[1] - here[1])),
            old[1] + ((above[0] - here[0]) - next_x(here[2])),
            old[2] + (next_x(here[1]) - next_y(here[0])),
        ]
        return [jnp.where(keep, f, 0.0) for f in out]

    def curl_p(here, below):
        return [
            prev_y(here[2]) - (here[1] - below[1]),
            (here[0] - below[0]) - prev_x(here[2]),
            prev_x(here[1]) - prev_y(here[0]),
        ]

    def flush(z):
        for c in range(3):
            at = pl.ds(c * cells + z * nx, nx * 2)
            for k, (source, target) in enumerate(((out_e, e_out), (out_h, h_out))):
                sem = sems.at[k * 3 + c]
                pltpu.make_async_copy(source.at[at, :], target.at[at, :], sem).start()

    zeros = jnp.zeros((rows, 128), jnp.float32)
    total = column[...]
    v_here = [load(V0 + c, -1) for c in range(3)]
    mag_below = [zeros] * 3
    mag_mid = mag2_below = inc_below = drv_below = None
    for z in range(-1, nz + 1):
        v_above = [load(V0 + c, z + 1) for c in range(3)] if z < nz else v_here
        old = [load(H0 + c, z) for c in range(3)]
        if z < 0:
            side_y, side_z = (zh[pl.ds(20 * nx + k, 1), :] for k in range(2))
            old[1] = old[1] - jnp.where(row == rows - 1, side_z, 0.0)
            old[2] = old[2] + jnp.where(row == rows - 1, side_y, 0.0)
        mag = magnetic(z, old, v_here, v_above)
        if z == nz:
            mag[0] = zeros
        v_here = v_above
        curl = curl_p(mag, mag_below)
        inc = [load(Q0 + c, z) - DT_STEP * curl[c] for c in range(3)]
        if z < 0:
            inc[0] = inc[0] + jnp.where(row == nx - 1, DT_STEP * beyond, 0.0)
        drive = load(DR, z)
        drv = [drive * f for f in inc]
        if 0 <= z < nz:
            cell = jnp.zeros((nx, 128), jnp.float32)
            for c in range(3):
                cell = cell + inc[c][:nx] * weight[pl.ds(c * cells + z * nx, nx), :]
            total = total + cell
        if z >= 0:
            low = z - 1
            mag2 = magnetic(low, mag_mid, drv_below, drv)
            if low >= 0:
                decay = work[pl.ds(DECAY * tall + (low + 1) * nx, nx), :]
                curl = curl_p(mag2, mag2_below)
                for c in range(3):
                    at = pl.ds(c * cells + low * nx, nx)
                    out_h[at, :] = mag2[c][:nx]
                    out_e[at, :] = decay * inc_below[c][:nx] - DT_STEP * curl[c][:nx]
                if low % 2 == 1:
                    flush(low - 1)
            mag2_below = mag2
        inc_below, drv_below = inc, drv
        mag_mid, mag_below = mag, mag

    devices = sums.shape[0]
    total = total * (-1.0 / layers)
    owner = B_DEV * lax.broadcasted_iota(jnp.int32, (devices, 128), 0)
    spot = lax.broadcasted_iota(jnp.int32, (devices, 128), 1)
    parts = [jnp.zeros((devices, 128), jnp.float32) for _ in range(B_DEV)]
    for group in range(nx // 4):
        four = jnp.sum(total[4 * group : 4 * group + 4], axis=0, keepdims=True)
        label = blocks[pl.ds(4 * group, 1), :]
        for k in range(B_DEV):
            parts[k] = parts[k] + jnp.where(label == owner + k, four, 0.0)
    packed = jnp.zeros((devices, 128), jnp.float32)
    for k in range(B_DEV):
        packed = jnp.where(spot == k, jnp.sum(parts[k], axis=1, keepdims=True), packed)
    sums[...] = packed

    for c in range(3):
        at = pl.ds(c * cells, cells)
        for k, (source, target) in enumerate(((out_e, e_out), (out_h, h_out))):
            pltpu.make_async_copy(source.at[at, :], target.at[at, :], sems.at[k * 3 + c]).wait()


def swap_pairs(count, offset):
    pairs = []
    for low in range(offset, count - 1, 2):
        pairs += [(low, low + 1), (low + 1, low)]
    return pairs


def estimate(flops, moved):
    return pl.CostEstimate(flops=flops, bytes_accessed=moved, transcendentals=0)


def on_device(
    adjoint_e, adjoint_h, source_e, e_saved, material_eps, material_id, pml_level, block_map
):
    nz, nx, ny = material_id.shape
    slabs, tiles = lax.axis_size("gz"), lax.axis_size("xy")
    cells, tall, deep = nz * nx, nx * (nz + 2), nz + 2
    field = cells * ny
    f32, bf16, i32 = jnp.float32, jnp.bfloat16, jnp.int32
    params = pltpu.CompilerParams(vmem_limit_bytes=24 * 1024 * 1024)
    raw = (material_eps, adjoint_e, adjoint_h, source_e, material_id, pml_level)
    raw = [pltpu.with_memory_space_constraint(a, pltpu.HBM) for a in raw]
    table = pltpu.SMEM(material_eps.shape, f32)
    z_msg, x_msg = shape_of(Z_SLOTS * nx, ny), shape_of(X_SLOTS * deep, ny)

    za, zb = pl.pallas_call(
        functools.partial(faces_kernel, nz, nx),
        out_shape=(z_msg, z_msg),
        in_specs=[HBM] * 6,
        out_specs=(VMEM,) * 2,
        scratch_shapes=[
            table,
            pltpu.VMEM((2, 3, 2, nx, ny), f32),
            pltpu.VMEM((2, 3, 2, nx, ny), f32),
            pltpu.VMEM((2, 3, 2, nx, ny), bf16),
            pltpu.VMEM((2, 2, nx, ny), i32),
            pltpu.VMEM((2, 2, nx, ny), i32),
            pltpu.SemaphoreType.DMA((11,)),
        ],
        compiler_params=params,
        cost_estimate=estimate(60 * field // 4, 4 * 4 * field),
        name="faces",
    )(*raw)

    za = lax.ppermute(za, "gz", swap_pairs(slabs, 0))
    zb = lax.ppermute(zb, "gz", swap_pairs(slabs, 1))

    work = pl.pallas_call(
        functools.partial(prepare_kernel, nz, nx),
        out_shape=shape_of(FIELDS * tall, ny),
        in_specs=[HBM] * 6,
        out_specs=VMEM,
        scratch_shapes=[
            table,
            pltpu.VMEM((nz, nx, ny), i32),
            pltpu.VMEM((nz, nx, ny), i32),
            pltpu.VMEM((3, nz, nx, ny), bf16),
            pltpu.VMEM((3, nz, nx, ny), f32),
            pltpu.VMEM((3, nz, nx, ny), f32),
            pltpu.SemaphoreType.DMA((6,)),
        ],
        compiler_params=params,
        cost_estimate=estimate(80 * field, 4 * 25 * field),
        name="prepare",
    )(*raw)

    zh, xa, xb = pl.pallas_call(
        functools.partial(columns_kernel, nz, nx),
        out_shape=(shape_of(20 * nx + 8, ny), x_msg, x_msg),
        in_specs=[VMEM] * 3,
        out_specs=(VMEM,) * 3,
        compiler_params=params,
        cost_estimate=estimate(4 * field, 4 * field),
        name="columns",
    )(za, zb, work)

    xa = lax.ppermute(xa, "xy", swap_pairs(tiles, 0))
    xb = lax.ppermute(xb, "xy", swap_pairs(tiles, 1))

    weight, column = pl.pallas_call(
        functools.partial(weight_kernel, nz, nx),
        out_shape=(shape_of(3 * cells, ny), shape_of(nx, ny)),
        in_specs=[VMEM] * 2,
        out_specs=(VMEM,) * 2,
        compiler_params=params,
        cost_estimate=estimate(40 * field, 4 * 12 * field),
        name="weights",
    )(e_saved.reshape(-1, ny), work)

    field_e, field_h, sums = pl.pallas_call(
        functools.partial(march_kernel, nz, nx, nz * slabs),
        out_shape=(shape_of(3 * cells, ny), shape_of(3 * cells, ny), shape_of(slabs * tiles, ny)),
        in_specs=[VMEM] * 7,
        out_specs=(HBM, HBM, VMEM),
        scratch_shapes=[
            pltpu.VMEM((10 * deep * 8, ny), f32),
            pltpu.VMEM((3 * cells, ny), f32),
            pltpu.VMEM((3 * cells, ny), f32),
            pltpu.SemaphoreType.DMA((6,)),
        ],
        compiler_params=params,
        cost_estimate=estimate(200 * field, 4 * 25 * field),
        name="march",
    )(work, zh, weight, column, xa, xb, block_map)

    gathered = lax.all_to_all(sums, ("gz", "xy"), 0, 0, tiled=True)
    design_grad = jnp.sum(gathered, axis=0)[:B_DEV]
    return field_e.reshape(adjoint_e.shape), field_h.reshape(adjoint_h.shape), design_grad


def solution(mesh):
    placed = (
        P(None, "gz", "xy", None),
        P(None, "gz", "xy", None),
        P(None, "gz", "xy", None),
        P(None, None, "gz", "xy", None),
        P(),
        P("gz", "xy", None),
        P("gz", "xy", None),
        P("xy", None),
    )
    return jax.shard_map(
        on_device,
        mesh=mesh,
        in_specs=placed,
        out_specs=(P(None, "gz", "xy", None), P(None, "gz", "xy", None), P(("gz", "xy"))),
        check_vma=False,
    )
```

time: 104 us -> 32 us (0.31)
  other arithmetic: 29 us -> 0.56 us
  blocking collectives: 42.1 us -> 20.1 us
  starting transfers between devices: 20.1 us -> 4.57 us
  waiting for transfers between devices: 6.57 us -> 1.28 us
  local copies, waits for them, and re-layouts: 4.72 us -> 0.01 us
  Pallas kernels: 0 us -> 4.48 us
    unnamed x1 -> x0, blocking collectives: 42.1 us -> none
    all_to_all x0 -> x1, blocking collectives: none -> 20.1 us  [on_device(): gathered = lax.all_to_all(sums, ('gz', 'xy'), 0, 0, tiled=True)]
    ppermute x8 -> x4, starting transfers between devices: 20.1 us -> 4.57 us  [the longest x1 2.61 us: on_device(): xa = lax.ppermute(xa, 'xy', swap_pairs(tiles, 0))]
    scatter-add x1 -> x0, other arithmetic: 14.8 us -> none  [on_device(): jax.ops.segment_sum(columns.reshape(-1), block_map.reshape(-1), num_segme...]
    div x2 -> x0, other arithmetic: 6.1 us -> none  [the longest x1 6.1 us: on_device(): decay = (1.0 - sigma) / (1.0 + sigma)]
    ppermute x8 -> x4, waiting for transfers between devices: 6.57 us -> 1.28 us  [the longest x1 1.27 us: on_device(): xa = lax.ppermute(xa, 'xy', swap_pairs(tiles, 0))]
    reduce_sum x2 -> x1, other arithmetic: 5.34 us -> 0.56 us  [on_device(): design_grad = jnp.sum(gathered, axis=0)[:B_DEV]]
    pallas_call x0 -> x5, Pallas kernels: none -> 4.48 us  [the longest x1 1.66 us: on_device(): pl.pallas_call(functools.partial(march_kernel, nz, nx, nz * slabs), out_s...]
  transfers between devices with their start and end apart: 8 -> 4, of which waited for: 2 -> 1; matrix products, arithmetic and copies ran while one was open for 20% -> 0% of each run, Pallas kernels for 0% -> 5%
where the time goes in v2:
time: 32 us; the launch traced here: 31.7 us
  blocking collectives  20.1 us (63%)
  starting transfers between devices  4.57 us (14%)
  Pallas kernels  4.48 us (14%)
  waiting for transfers between devices  1.28 us (4%)
  between operations  0.72 us (2%)
  other arithmetic  0.56 us (2%)
    all_to_all x1, blocking collectives, on_device(): gathered = lax.all_to_all(sums, ('gz', 'xy'), 0, 0, tiled=True)  20.1 us
    ppermute x1, starting transfers between devices, on_device(): xa = lax.ppermute(xa, 'xy', swap_pairs(tiles, 0))  2.61 us
    pallas_call x1, Pallas kernels, on_device(): pl.pallas_call(functools.partial(march_kernel, nz, nx, nz * slabs), out_s...  1.66 us
    pallas_call x1, Pallas kernels, on_device(): pl.pallas_call(functools.partial(prepare_kernel, nz, nx), out_shape=shape...  1.42 us
    ppermute x1, waiting for transfers between devices, on_device(): xa = lax.ppermute(xa, 'xy', swap_pairs(tiles, 0))  1.27 us
    pallas_call x1, Pallas kernels, on_device(): pl.pallas_call(functools.partial(faces_kernel, nz, nx), out_shape=(z_msg,...  1.1 us
    ppermute x1, starting transfers between devices, on_device(): zb = lax.ppermute(zb, 'gz', swap_pairs(slabs, 1))  0.78 us
    ppermute x1, starting transfers between devices, on_device(): xb = lax.ppermute(xb, 'xy', swap_pairs(tiles, 1))  0.65 us
  transfers between devices with their start and end apart: 4, of which 1 were waited for; matrix products, arithmetic and copies ran while one was open for 0% of the time, Pallas kernels for 5%

profile of v2, /device:TPU:0, one launch (start us, length us, event | category | flops | bytes accessed | tf_op | source)
XLA Modules:
  0.0 31.7 jit_solution(2201898670837143299)
XLA Ops:
  0.6 1.1 %faces.1 = (f32[128,128]{1,0:T(8,128)S(1)}, f32[128,128]{1,0:T(8,128)S(1)}) custom-call(f32[8]{0:T(128)} %eps_in.3, f32[3,14,16,128]{3,2,1,0:T(8,128)} %e_in.3, f32[3,14,16,128]{3,2,1,0:T(8,128)} %h_in.3, bf16[3,14,16,128]{3,2,1,0:T(8,128)(2,1)} %s_in.3, s32[14,16,128]{2,1,0:T(8,128)} %mat_in.3, s32[14,16,128]{2,1,0:T(8,128)} %pml_in.3), custom_call_target="tpu_custom_call" | custom-call | flops 430080 | bytes 458752 | tf_op jit(solution)/shard_map/faces/pallas_call | solution.py:417
  1.7 0.5 %collective-permute-start = (f32[128,128]{1,0:T(8,128)S(1)}, f32[128,128]{1,0:T(8,128)S(1)}, u32[]{:S(2)}, u32[]{:S(2)}) collective-permute-start(f32[128,128]{1,0:T(8,128)S(1)} %get-tuple-element.13), channel_id=1, source_target_pairs={{0,8},{8,0},{16,24},{24,16},{1,9},{9,1},{17,25},{25,17},{2,10},{10... | collective-permute-start | bytes 196616 | tf_op jit(solution)/shard_map/ppermute | solution.py:436
  2.3 0.0 copy-start
  2.3 0.8 %collective-permute-start.1 = (f32[128,128]{1,0:T(8,128)S(1)}, f32[128,128]{1,0:T(8,128)S(1)}, u32[]{:S(2)}, u32[]{:S(2)}) collective-permute-start(f32[128,128]{1,0:T(8,128)S(1)} %get-tuple-element.14), channel_id=1, source_target_pairs={{8,16},{16,8},{9,17},{17,9},{10,18},{18,10},{11,19},{19,11},{12,20... | collective-permute-start | bytes 196616 | tf_op jit(solution)/shard_map/ppermute | solution.py:437
  3.1 1.4 %prepare.1.work = f32[3840,128]{1,0:T(8,128)S(1)} custom-call(f32[8]{0:T(128)} %eps_in.3, f32[3,14,16,128]{3,2,1,0:T(8,128)} %e_in.3, f32[3,14,16,128]{3,2,1,0:T(8,128)} %h_in.3, bf16[3,14,16,128]{3,2,1,0:T(8,128)(2,1)} %s_in.3, s32[14,16,128]{2,1,0:T(8,128)} %mat_in.3, s32[14,16,128]{2,1,0:T(8,128)} %pml_in.3), custom_call_target="tpu_custom_call" | custom-call | flops 2293760 | bytes 2867200 | tf_op jit(solution)/shard_map/prepare/pallas_call | solution.py:439
  4.5 0.0 copy-start.1
  4.5 0.0 collective-permute-done.za
  4.5 0.0 collective-permute-done.1.zb
  4.5 0.2 columns.1
  4.7 2.6 %collective-permute-start.2 = (f32[96,128]{1,0:T(8,128)S(1)}, f32[96,128]{1,0:T(8,128)S(1)}, u32[]{:S(2)}, u32[]{:S(2)}) collective-permute-start(f32[96,128]{1,0:T(8,128)S(1)} %get-tuple-element.18), channel_id=1, source_target_pairs={{0,1},{1,0},{2,3},{3,2},{4,5},{5,4},{6,7},{7,6},{8,9},{9,8},{10,11... | collective-permute-start | bytes 147464 | tf_op jit(solution)/shard_map/ppermute | solution.py:468
  7.3 0.7 %collective-permute-start.3 = (f32[96,128]{1,0:T(8,128)S(1)}, f32[96,128]{1,0:T(8,128)S(1)}, u32[]{:S(2)}, u32[]{:S(2)}) collective-permute-start(f32[96,128]{1,0:T(8,128)S(1)} %get-tuple-element.19), channel_id=1, source_target_pairs={{1,2},{2,1},{3,4},{4,3},{5,6},{6,5},{9,10},{10,9},{11,12},{12,11},... | collective-permute-start | bytes 147464 | tf_op jit(solution)/shard_map/ppermute | solution.py:469
  8.0 0.0 copy-done
  8.0 0.1 weights.1
  8.1 1.3 %collective-permute-done.2.xa = f32[96,128]{1,0:T(8,128)S(1)} collective-permute-done((f32[96,128]{1,0:T(8,128)S(1)}, f32[96,128]{1,0:T(8,128)S(1)}, u32[]{:S(2)}, u32[]{:S(2)}) %collective-permute-start.2) | collective-permute-done | bytes 49184 | tf_op jit(solution)/shard_map/ppermute | solution.py:468
  9.4 0.0 collective-permute-done.3.xb
  9.4 0.0 copy-done.1
  9.4 1.7 %march.1 = (f32[672,128]{1,0:T(8,128)}, f32[672,128]{1,0:T(8,128)}, f32[32,128]{1,0:T(8,128)S(1)}) custom-call(f32[3840,128]{1,0:T(8,128)S(1)} %prepare.1.work, f32[328,128]{1,0:T(8,128)S(1)} %get-tuple-element.15.zh, f32[672,128]{1,0:T(8,128)S(1)} %get-tuple-element.16.weight, f32[16,128]{1,0:T(8,128)S(1)} %get-tuple-element.17.column, ...), custom_call_target="tpu_custom_call" | custom-call | flops 5734400 | bytes 2867200 | tf_op jit(solution)/shard_map/march/pallas_call | solution.py:481
  11.1 20.1 %all_to_all.9 = f32[32,1,128]{2,1,0:T(1,128)S(1)} all-to-all(f32[32,1,128]{2,1,0:T(1,128)S(1)} %bitcast.8), channel_id=1, replica_groups=mesh['gz'=4,'xy'=8] {'gz','xy'}, dimensions={0} | all-to-all | bytes 32768 | tf_op jit(solution)/shard_map/all_to_all | solution.py:497
  31.1 0.6 %reduce_sum.9 = f32[128]{0:T(128)} reduce(f32[32,1,128]{2,1,0:T(1,128)S(1)} %all_to_all.9, f32[]{:T(128)} %constant.0.clone.1), dimensions={0,1}, to_apply=%region_0.0 | reduce | flops 3968 | bytes 16900 | tf_op jit(solution)/shard_map/reduce_sum | solution.py:498
Async XLA Ops:
  1.7 2.8 %collective-permute-start = (f32[128,128]{1,0:T(8,128)S(1)}, f32[128,128]{1,0:T(8,128)S(1)}, u32[]{:S(2)}, u32[]{:S(2)}) collective-permute-start(f32[128,128]{1,0:T(8,128)S(1)} %get-tuple-element.13), channel_id=1, source_target_pairs={{0,8},{8,0},{16,24},{24,16},{1,9},{9,1},{17,25},{25,17},{2,10},{10... | collective-permute-start | bytes 196616 | tf_op jit(solution)/shard_map/ppermute | solution.py:436
  2.3 5.7 %copy-start = (bf16[3,3,14,16,128]{4,3,2,1,0:T(8,128)(2,1)S(1)}, bf16[3,3,14,16,128]{4,3,2,1,0:T(8,128)(2,1)}, u32[]{:S(2)}) copy-start(bf16[3,3,14,16,128]{4,3,2,1,0:T(8,128)(2,1)} %param.11) | copy-start | bytes 1548292
  2.3 2.2 %collective-permute-start.1 = (f32[128,128]{1,0:T(8,128)S(1)}, f32[128,128]{1,0:T(8,128)S(1)}, u32[]{:S(2)}, u32[]{:S(2)}) collective-permute-start(f32[128,128]{1,0:T(8,128)S(1)} %get-tuple-element.14), channel_id=1, source_target_pairs={{8,16},{16,8},{9,17},{17,9},{10,18},{18,10},{11,19},{19,11},{12,20... | collective-permute-start | bytes 196616 | tf_op jit(solution)/shard_map/ppermute | solution.py:437
  4.5 4.9 %copy-start.1 = (s32[16,128]{1,0:T(8,128)S(1)}, s32[16,128]{1,0:T(8,128)}, u32[]{:S(2)}) copy-start(s32[16,128]{1,0:T(8,128)} %blocks.1) | copy-start | bytes 24580
  4.7 4.7 %collective-permute-start.2 = (f32[96,128]{1,0:T(8,128)S(1)}, f32[96,128]{1,0:T(8,128)S(1)}, u32[]{:S(2)}, u32[]{:S(2)}) collective-permute-start(f32[96,128]{1,0:T(8,128)S(1)} %get-tuple-element.18), channel_id=1, source_target_pairs={{0,1},{1,0},{2,3},{3,2},{4,5},{5,4},{6,7},{7,6},{8,9},{9,8},{10,11... | collective-permute-start | bytes 147464 | tf_op jit(solution)/shard_map/ppermute | solution.py:468
  7.3 2.1 %collective-permute-start.3 = (f32[96,128]{1,0:T(8,128)S(1)}, f32[96,128]{1,0:T(8,128)S(1)}, u32[]{:S(2)}, u32[]{:S(2)}) collective-permute-start(f32[96,128]{1,0:T(8,128)S(1)} %get-tuple-element.19), channel_id=1, source_target_pairs={{1,2},{2,1},{3,4},{4,3},{5,6},{6,5},{9,10},{10,9},{11,12},{12,11},... | collective-permute-start | bytes 147464 | tf_op jit(solution)/shard_map/ppermute | solution.py:469

commit v3 on v2

--- a/solution.py
+++ b/solution.py
@@ -59,7 +59,7 @@
     return (1.0 - sigma) * recip, DT_STEP * inv * recip, inv
 
 
-def faces_kernel(nz, nx, eps_in, e_in, h_in, s_in, mat_in, pml_in, za, zb, eps, *rest):
+def faces_kernel(nz, nx, eps_in, e_in, h_in, s_in, mat_in, pml_in, zb, za, eps, *rest):
     bufs, sems = rest[:-1], rest[-1]
     copies = [pltpu.make_async_copy(eps_in, eps, sems.at[0])]
     for k, ref in enumerate((e_in, h_in, s_in, mat_in, pml_in)):
@@ -153,7 +153,7 @@
             work[pl.ds((H0 + c) * tall + (z + 1) * nx, nx), :] = h[c, z]
 
 
-def columns_kernel(nz, nx, za, zb, work, zh, xa, xb):
+def columns_kernel(nz, nx, zb, za, work, zh, xb, xa):
     tall = nx * (nz + 2)
     deep = nz + 2
     zero = jnp.zeros((nx, 128), jnp.float32)
@@ -237,28 +237,113 @@
     either(is_odd("xy"), put, xa, xb)
 
 
-def weight_kernel(nz, nx, saved, work, weight, column):
+def spread(fours, groups, blocks, shape):
+    owner = lax.broadcasted_iota(jnp.int32, shape, 0)
+    out = jnp.zeros(shape, jnp.float32)
+    for four, group in zip(fours, groups):
+        out = out + jnp.where(blocks[pl.ds(4 * group, 1), :] == owner, four, 0.0)
+    return out
+
+
+def interior_kernel(nz, nx, layers, saved, work, zh, blocks, partial, edges, weight):
     cells, tall = nz * nx, nx * (nz + 2)
+    row, first, last = masks(nx)
+    above_edge = jnp.broadcast_to(lax.axis_index("gz"), row.shape) > 0
+
+    def load(field, z):
+        if 0 <= z < nz:
+            return work[pl.ds(field * tall + (z + 1) * nx, nx), :]
+        return zh[pl.ds((2 * field + (z > 0)) * nx, nx), :]
+
+    def next_y(f):
+        return jnp.where(last, 0.0, pltpu.roll(f, 127, 1)) - f
+
+    def prev_y(f):
+        return f - jnp.where(first, 0.0, pltpu.roll(f, 1, 1))
+
+    def next_x(f):
+        return jnp.where(row == nx - 1, 0.0, pltpu.roll(f, nx - 1, 0)) - f
+
+    def prev_x(f):
+        return f - jnp.where(row == 0, 0.0, pltpu.roll(f, 1, 0))
+
     total = jnp.zeros((nx, 128), jnp.float32)
-    for z in range(nz):
-        near = pl.ds(DECAY * tall + (z + 1) * nx, nx)
-        decay = work[near, :]
-        inv = work[pl.ds(INV * tall + (z + 1) * nx, nx), :]
-        cell = jnp.zeros((nx, 128), jnp.float32)
+    here = [load(V0 + c, -1) for c in range(3)]
+    below = None
+    for z in range(-1, nz):
+        above = [load(V0 + c, z + 1) for c in range(3)]
+        mag = [
+            load(H0, z) + (next_y(here[2]) - (above[1] - here[1])),
+            load(H1, z) + ((above[0] - here[0]) - next_x(here[2])),
+        ]
+        if z < 0:
+            mag = [jnp.where(above_edge, f, 0.0) for f in mag]
+        else:
+            mag.append(load(H2, z) + (next_x(here[1]) - next_y(here[0])))
+            curl = [
+                prev_y(mag[2]) - (mag[1] - below[1]),
+                (mag[0] - below[0]) - prev_x(mag[2]),
+                prev_x(mag[1]) - prev_y(mag[0]),
+            ]
+            decay, inv = load(DECAY, z), load(INV, z)
+            cell = jnp.zeros((nx, 128), jnp.float32)
+            for c in range(3):
+                times = [
+                    saved[pl.ds((3 * t + c) * cells + z * nx, nx), :].astype(jnp.float32)
+                    for t in range(3)
+                ]
+                factor = times[1] - decay * times[0]
+                weight[pl.ds(c * tall + (z + 1) * nx, nx), :] = factor * inv
+                cell = cell + load(I0 + c, z) * (times[2] - decay * times[1])
+                cell = cell + (load(Q0 + c, z) - DT_STEP * curl[c]) * factor
+            total = total + cell * inv
+        here, below = above, mag
+    total = total * (-1.0 / layers)
+    fours = [
+        jnp.sum(total[4 * k : 4 * k + 4], axis=0, keepdims=True) for k in range(nx // 4)
+    ]
+    partial[...] = spread(fours, range(nx // 4), blocks, partial.shape)
+    for side, x in enumerate((0, nx - 1)):
         for c in range(3):
-            times = [
-                saved[pl.ds((3 * t + c) * cells + z * nx, nx), :].astype(jnp.float32)
-                for t in range(3)
-            ]
-            incoming = work[pl.ds((I0 + c) * tall + (z + 1) * nx, nx), :]
-            cell = cell + incoming * (times[2] - decay * times[1])
-            weight[pl.ds(c * cells + z * nx, nx), :] = (times[1] - decay * times[0]) * inv
-        total = total + cell * inv
-    column[...] = total
+            part = weight[pl.ds(c * tall + nx + x, nz, stride=nx), :]
+            edges[pl.ds((3 * side + c) * (nz + 2) + 1, nz), :] = part
+
+
+def edge_kernel(nz, nx, layers, work, partial, edges, blocks, xb, xa, sums):
+    tall, deep = nx * (nz + 2), nz + 2
+    row, first, last = masks(deep)
+    odd_x = jnp.broadcast_to(is_odd("xy"), row.shape)
+    own = jnp.logical_and(row > 0, row < deep - 1)
+    low_side = jnp.logical_and(own, jnp.broadcast_to(lax.axis_index("xy"), row.shape) > 0)
+
+    def slot(slots, field):
+        at = pl.ds(slots.index(field) * deep, deep)
+        return jnp.where(odd_x, xa[at, :], xb[at, :]), jnp.where(odd_x, xb[at, :], xa[at, :])
+
+    def prev_y(f):
+        return f - jnp.where(first, 0.0, pltpu.roll(f, 1, 1))
+
+    def factor(side, c):
+        return edges[pl.ds((3 * side + c) * deep, deep), :]
+
+    mag_y = slot(X_LOW, H1)[0] - work[pl.ds(V2 * tall, deep, stride=nx), :]
+    mag_z = slot(X_LOW, H2)[0] + work[pl.ds(V1 * tall, deep, stride=nx), :]
+    near = DT_STEP * (mag_y * factor(0, 2) - mag_z * factor(0, 1))
+    v_y, v_z = slot(X_HIGH, V1)[1], slot(X_HIGH, V2)[1]
+    far = DT_STEP * (
+        v_y * factor(1, 1)
+        + v_z * factor(1, 2)
+        - (prev_y(v_y) + (v_z - pltpu.roll(v_z, 1, 0))) * factor(1, 0)
+    )
+    near = jnp.sum(jnp.where(low_side, near, 0.0), axis=0, keepdims=True)
+    far = jnp.sum(jnp.where(own, far, 0.0), axis=0, keepdims=True)
+
+    ends = (near * (-1.0 / layers), far * (-1.0 / layers))
+    sums[...] = partial[...] + spread(ends, (0, nx // 4 - 1), blocks, sums.shape)
 
 
 def march_kernel(
-    nz, nx, layers, work, zh, weight, column, xa, xb, blocks, e_out, h_out, sums, xh, out_e, out_h, sems
+    nz, nx, work, zh, xb, xa, e_out, h_out, xh, out_e, out_h, sems
 ):
     cells, tall, deep = nz * nx, nx * (nz + 2), nz + 2
     index_z, index_x = lax.axis_index("gz"), lax.axis_index("xy")
@@ -326,7 +411,6 @@
                 pltpu.make_async_copy(source.at[at, :], target.at[at, :], sem).start()
 
     zeros = jnp.zeros((rows, 128), jnp.float32)
-    total = column[...]
     v_here = [load(V0 + c, -1) for c in range(3)]
     mag_below = [zeros] * 3
     mag_mid = mag2_below = inc_below = drv_below = None
@@ -347,11 +431,6 @@
             inc[0] = inc[0] + jnp.where(row == nx - 1, DT_STEP * beyond, 0.0)
         drive = load(DR, z)
         drv = [drive * f for f in inc]
-        if 0 <= z < nz:
-            cell = jnp.zeros((nx, 128), jnp.float32)
-            for c in range(3):
-                cell = cell + inc[c][:nx] * weight[pl.ds(c * cells + z * nx, nx), :]
-            total = total + cell
         if z >= 0:
             low = z - 1
             mag2 = magnetic(low, mag_mid, drv_below, drv)
@@ -368,21 +447,6 @@
         inc_below, drv_below = inc, drv
         mag_mid, mag_below = mag, mag
 
-    devices = sums.shape[0]
-    total = total * (-1.0 / layers)
-    owner = B_DEV * lax.broadcasted_iota(jnp.int32, (devices, 128), 0)
-    spot = lax.broadcasted_iota(jnp.int32, (devices, 128), 1)
-    parts = [jnp.zeros((devices, 128), jnp.float32) for _ in range(B_DEV)]
-    for group in range(nx // 4):
-        four = jnp.sum(total[4 * group : 4 * group + 4], axis=0, keepdims=True)
-        label = blocks[pl.ds(4 * group, 1), :]
-        for k in range(B_DEV):
-            parts[k] = parts[k] + jnp.where(label == owner + k, four, 0.0)
-    packed = jnp.zeros((devices, 128), jnp.float32)
-    for k in range(B_DEV):
-        packed = jnp.where(spot == k, jnp.sum(parts[k], axis=1, keepdims=True), packed)
-    sums[...] = packed
-
     for c in range(3):
         at = pl.ds(c * cells, cells)
         for k, (source, target) in enumerate(((out_e, e_out), (out_h, h_out))):
@@ -406,6 +470,7 @@
     nz, nx, ny = material_id.shape
     slabs, tiles = lax.axis_size("gz"), lax.axis_size("xy")
     cells, tall, deep = nz * nx, nx * (nz + 2), nz + 2
+    blocks = B_DEV * slabs * tiles
     field = cells * ny
     f32, bf16, i32 = jnp.float32, jnp.bfloat16, jnp.int32
     params = pltpu.CompilerParams(vmem_limit_bytes=24 * 1024 * 1024)
@@ -414,7 +479,7 @@
     table = pltpu.SMEM(material_eps.shape, f32)
     z_msg, x_msg = shape_of(Z_SLOTS * nx, ny), shape_of(X_SLOTS * deep, ny)
 
-    za, zb = pl.pallas_call(
+    zb, za = pl.pallas_call(
         functools.partial(faces_kernel, nz, nx),
         out_shape=(z_msg, z_msg),
         in_specs=[HBM] * 6,
@@ -433,8 +498,8 @@
         name="faces",
     )(*raw)
 
+    zb = lax.ppermute(zb, "gz", swap_pairs(slabs, 1))
     za = lax.ppermute(za, "gz", swap_pairs(slabs, 0))
-    zb = lax.ppermute(zb, "gz", swap_pairs(slabs, 1))
 
     work = pl.pallas_call(
         functools.partial(prepare_kernel, nz, nx),
@@ -455,7 +520,7 @@
         name="prepare",
     )(*raw)
 
-    zh, xa, xb = pl.pallas_call(
+    zh, xb, xa = pl.pallas_call(
         functools.partial(columns_kernel, nz, nx),
         out_shape=(shape_of(20 * nx + 8, ny), x_msg, x_msg),
         in_specs=[VMEM] * 3,
@@ -463,26 +528,39 @@
         compiler_params=params,
         cost_estimate=estimate(4 * field, 4 * field),
         name="columns",
-    )(za, zb, work)
-
+    )(zb, za, work)
+
+    xb = lax.ppermute(xb, "xy", swap_pairs(tiles, 1))
     xa = lax.ppermute(xa, "xy", swap_pairs(tiles, 0))
-    xb = lax.ppermute(xb, "xy", swap_pairs(tiles, 1))
-
-    weight, column = pl.pallas_call(
-        functools.partial(weight_kernel, nz, nx),
-        out_shape=(shape_of(3 * cells, ny), shape_of(nx, ny)),
-        in_specs=[VMEM] * 2,
+
+    partial, edges = pl.pallas_call(
+        functools.partial(interior_kernel, nz, nx, nz * slabs),
+        out_shape=(shape_of(blocks, ny), shape_of(6 * deep, ny)),
+        in_specs=[VMEM] * 4,
         out_specs=(VMEM,) * 2,
+        scratch_shapes=[pltpu.VMEM((3 * tall, ny), f32)],
         compiler_params=params,
-        cost_estimate=estimate(40 * field, 4 * 12 * field),
-        name="weights",
-    )(e_saved.reshape(-1, ny), work)
-
-    field_e, field_h, sums = pl.pallas_call(
-        functools.partial(march_kernel, nz, nx, nz * slabs),
-        out_shape=(shape_of(3 * cells, ny), shape_of(3 * cells, ny), shape_of(slabs * tiles, ny)),
-        in_specs=[VMEM] * 7,
-        out_specs=(HBM, HBM, VMEM),
+        cost_estimate=estimate(150 * field, 4 * 20 * field),
+        name="interior",
+    )(e_saved.reshape(-1, ny), work, zh, block_map)
+
+    sums = pl.pallas_call(
+        functools.partial(edge_kernel, nz, nx, nz * slabs),
+        out_shape=shape_of(blocks, ny),
+        in_specs=[VMEM] * 6,
+        out_specs=VMEM,
+        compiler_params=params,
+        cost_estimate=estimate(4 * field, 4 * field),
+        name="edges",
+    )(work, partial, edges, block_map, xb, xa)
+
+    gathered = lax.all_to_all(sums, ("gz", "xy"), 0, 0, tiled=True)
+
+    field_e, field_h = pl.pallas_call(
+        functools.partial(march_kernel, nz, nx),
+        out_shape=(shape_of(3 * cells, ny), shape_of(3 * cells, ny)),
+        in_specs=[VMEM] * 4,
+        out_specs=(HBM, HBM),
         scratch_shapes=[
             pltpu.VMEM((10 * deep * 8, ny), f32),
             pltpu.VMEM((3 * cells, ny), f32),
@@ -492,10 +570,10 @@
         compiler_params=params,
         cost_estimate=estimate(200 * field, 4 * 25 * field),
         name="march",
-    )(work, zh, weight, column, xa, xb, block_map)
+    )(work, zh, xb, xa)
 
     gathered = lax.all_to_all(sums, ("gz", "xy"), 0, 0, tiled=True)
-    design_grad = jnp.sum(gathered, axis=0)[:B_DEV]
+    design_grad = jnp.sum(gathered.reshape(-1, B_DEV, ny), axis=(0, 2))
     return field_e.reshape(adjoint_e.shape), field_h.reshape(adjoint_h.shape), design_grad
 
 

time: 32 us -> 30.2 us (0.944)
  blocking collectives: 20.1 us -> 0 us
  starting transfers between devices: 4.57 us -> 15.9 us
  waiting for transfers between devices: 1.28 us -> 7.34 us
  Pallas kernels: 4.48 us -> 5.29 us
    all_to_all x1 -> x0, blocking collectives: 20.1 us -> none  [on_device(): gathered = lax.all_to_all(sums, ('gz', 'xy'), 0, 0, tiled=True)]
    all_to_all x0 -> x1, starting transfers between devices: none -> 5.83 us  [on_device(): gathered = lax.all_to_all(sums, ('gz', 'xy'), 0, 0, tiled=True)]
    all_to_all x0 -> x1, waiting for transfers between devices: none -> 5.67 us  [on_device(): gathered = lax.all_to_all(sums, ('gz', 'xy'), 0, 0, tiled=True)]
    ppermute x1, starting transfers between devices: 0.53 us -> 4.36 us  [on_device(): za = lax.ppermute(za, 'gz', swap_pairs(slabs, 0))]
    ppermute x1, starting transfers between devices: 2.61 us -> 4.38 us  [on_device(): xa = lax.ppermute(xa, 'xy', swap_pairs(tiles, 0))]
    pallas_call x2 -> x3, Pallas kernels: 1.78 us -> 2.6 us  [the longest x1 1.51 us: on_device(): pl.pallas_call(functools.partial(march_kernel, nz, nx), out_shape=(shape_...]
    ppermute x1, waiting for transfers between devices: 1.27 us -> 1.67 us  [on_device(): xa = lax.ppermute(xa, 'xy', swap_pairs(tiles, 0))]
  transfers between devices with their start and end apart: 4 -> 5, of which waited for: 1 -> 2; matrix products, arithmetic and copies ran while one was open for 0% -> 0% of each run, Pallas kernels for 5% -> 11%
where the time goes in v3:
time: 30.2 us; the launch traced here: 29.9 us
  starting transfers between devices  15.9 us (53%)
  waiting for transfers between devices  7.34 us (24%)
  Pallas kernels  5.29 us (18%)
  between operations  0.73 us (2%)
  other arithmetic  0.66 us (2%)
    all_to_all x1, starting transfers between devices, on_device(): gathered = lax.all_to_all(sums, ('gz', 'xy'), 0, 0, tiled=True)  5.83 us
    all_to_all x1, waiting for transfers between devices, on_device(): gathered = lax.all_to_all(sums, ('gz', 'xy'), 0, 0, tiled=True)  5.67 us
    ppermute x1, starting transfers between devices, on_device(): xa = lax.ppermute(xa, 'xy', swap_pairs(tiles, 0))  4.38 us
    ppermute x1, starting transfers between devices, on_device(): za = lax.ppermute(za, 'gz', swap_pairs(slabs, 0))  4.36 us
    ppermute x1, waiting for transfers between devices, on_device(): xa = lax.ppermute(xa, 'xy', swap_pairs(tiles, 0))  1.67 us
    pallas_call x1, Pallas kernels, on_device(): pl.pallas_call(functools.partial(march_kernel, nz, nx), out_shape=(shape_...  1.51 us
    pallas_call x1, Pallas kernels, on_device(): pl.pallas_call(functools.partial(prepare_kernel, nz, nx), out_shape=shape...  1.41 us
    pallas_call x1, Pallas kernels, on_device(): pl.pallas_call(functools.partial(faces_kernel, nz, nx), out_shape=(z_msg,...  1.1 us
  transfers between devices with their start and end apart: 5, of which 2 were waited for; matrix products, arithmetic and copies ran while one was open for 0% of the time, Pallas kernels for 11%

profile of v3, /device:TPU:0, one launch (start us, length us, event | category | flops | bytes accessed | tf_op | source)
XLA Modules:
  0.0 29.9 jit_solution(13109750843511100609)
XLA Ops:
  0.6 1.1 %faces.1 = (f32[128,128]{1,0:T(8,128)S(1)}, f32[128,128]{1,0:T(8,128)S(1)}) custom-call(f32[8]{0:T(128)} %eps_in.3, f32[3,14,16,128]{3,2,1,0:T(8,128)} %e_in.3, f32[3,14,16,128]{3,2,1,0:T(8,128)} %h_in.3, bf16[3,14,16,128]{3,2,1,0:T(8,128)(2,1)} %s_in.3, s32[14,16,128]{2,1,0:T(8,128)} %mat_in.3, s32[14,16,128]{2,1,0:T(8,128)} %pml_in.3), custom_call_target="tpu_custom_call" | custom-call | flops 430080 | bytes 458752 | tf_op jit(solution)/shard_map/faces/pallas_call | solution.py:482
  1.7 0.7 %collective-permute-start = (f32[128,128]{1,0:T(8,128)S(1)}, f32[128,128]{1,0:T(8,128)S(1)}, u32[]{:S(2)}, u32[]{:S(2)}) collective-permute-start(f32[128,128]{1,0:T(8,128)S(1)} %get-tuple-element.12), channel_id=1, source_target_pairs={{8,16},{16,8},{9,17},{17,9},{10,18},{18,10},{11,19},{19,11},{12,20... | collective-permute-start | bytes 196616 | tf_op jit(solution)/shard_map/ppermute | solution.py:501
  2.4 0.0 copy-start
  2.4 0.0 copy-start.1
  2.4 4.4 %collective-permute-start.1 = (f32[128,128]{1,0:T(8,128)S(1)}, f32[128,128]{1,0:T(8,128)S(1)}, u32[]{:S(2)}, u32[]{:S(2)}) collective-permute-start(f32[128,128]{1,0:T(8,128)S(1)} %get-tuple-element.13), channel_id=1, source_target_pairs={{0,8},{8,0},{16,24},{24,16},{1,9},{9,1},{17,25},{25,17},{2,10},{10... | collective-permute-start | bytes 196616 | tf_op jit(solution)/shard_map/ppermute | solution.py:502
  6.8 1.4 %prepare.1.work = f32[3840,128]{1,0:T(8,128)S(1)} custom-call(f32[8]{0:T(128)} %eps_in.3, f32[3,14,16,128]{3,2,1,0:T(8,128)} %e_in.3, f32[3,14,16,128]{3,2,1,0:T(8,128)} %h_in.3, bf16[3,14,16,128]{3,2,1,0:T(8,128)(2,1)} %s_in.3, s32[14,16,128]{2,1,0:T(8,128)} %mat_in.3, s32[14,16,128]{2,1,0:T(8,128)} %pml_in.3), custom_call_target="tpu_custom_call" | custom-call | flops 2293760 | bytes 2867200 | tf_op jit(solution)/shard_map/prepare/pallas_call | solution.py:504
  8.2 0.0 collective-permute-done.zb
  8.2 0.0 collective-permute-done.1.za
  8.2 0.2 columns.1
  8.4 0.7 %collective-permute-start.2 = (f32[96,128]{1,0:T(8,128)S(1)}, f32[96,128]{1,0:T(8,128)S(1)}, u32[]{:S(2)}, u32[]{:S(2)}) collective-permute-start(f32[96,128]{1,0:T(8,128)S(1)} %get-tuple-element.15), channel_id=1, source_target_pairs={{1,2},{2,1},{3,4},{4,3},{5,6},{6,5},{9,10},{10,9},{11,12},{12,11},... | collective-permute-start | bytes 147464 | tf_op jit(solution)/shard_map/ppermute | solution.py:533
  9.1 4.4 %collective-permute-start.3 = (f32[96,128]{1,0:T(8,128)S(1)}, f32[96,128]{1,0:T(8,128)S(1)}, u32[]{:S(2)}, u32[]{:S(2)}) collective-permute-start(f32[96,128]{1,0:T(8,128)S(1)} %get-tuple-element.16), channel_id=1, source_target_pairs={{0,1},{1,0},{2,3},{3,2},{4,5},{5,4},{6,7},{7,6},{8,9},{9,8},{10,11... | collective-permute-start | bytes 147464 | tf_op jit(solution)/shard_map/ppermute | solution.py:534
  13.5 0.0 copy-done
  13.5 0.0 copy-done.1
  13.5 0.4 %interior.1 = (f32[64,128]{1,0:T(8,128)S(1)}, f32[96,128]{1,0:T(8,128)S(1)}) custom-call(bf16[2016,128]{1,0:T(8,128)(2,1)S(1)} %bitcast.4, f32[3840,128]{1,0:T(8,128)S(1)} %prepare.1.work, f32[328,128]{1,0:T(8,128)S(1)} %get-tuple-element.14.zh, s32[16,128]{1,0:T(8,128)S(1)} %copy-done.1), custom_call_target="tpu_custom_call" | custom-call | flops 4300800 | bytes 2293760 | tf_op jit(solution)/shard_map/interior/pallas_call | solution.py:536
  13.9 0.0 collective-permute-done.2.xb
  13.9 1.7 %collective-permute-done.3.xa = f32[96,128]{1,0:T(8,128)S(1)} collective-permute-done((f32[96,128]{1,0:T(8,128)S(1)}, f32[96,128]{1,0:T(8,128)S(1)}, u32[]{:S(2)}, u32[]{:S(2)}) %collective-permute-start.3) | collective-permute-done | bytes 49184 | tf_op jit(solution)/shard_map/ppermute | solution.py:534
  15.5 0.7 %edges.1 = f32[64,128]{1,0:T(8,128)} custom-call(f32[3840,128]{1,0:T(8,128)S(1)} %prepare.1.work, f32[64,128]{1,0:T(8,128)S(1)} %get-tuple-element.19.partial, f32[96,128]{1,0:T(8,128)S(1)} %get-tuple-element.20.edges, s32[16,128]{1,0:T(8,128)S(1)} %copy-done.1, f32[96,128]{1,0:T(8,128)S(1)} %collective-permute-done.2.xb, ...), custom_call_target="tpu_custom_call" | custom-call | flops 114688 | bytes 114688 | tf_op jit(solution)/shard_map/edges/pallas_call | solution.py:547
  16.3 5.8 %all-to-all-start = ((f32[32,2,128]{2,1,0:T(2,128)}), f32[32,2,128]{2,1,0:T(2,128)S(1)}, u32[]{:S(2)}, u32[]{:S(2)}) async-start(f32[32,2,128]{2,1,0:T(2,128)} %bitcast.3), calls=%async_computation | async-start | bytes 65536 | tf_op jit(solution)/shard_map/all_to_all | solution.py:575
  22.1 1.5 %march.1 = (f32[672,128]{1,0:T(8,128)}, f32[672,128]{1,0:T(8,128)}) custom-call(f32[3840,128]{1,0:T(8,128)S(1)} %prepare.1.work, f32[328,128]{1,0:T(8,128)S(1)} %get-tuple-element.14.zh, f32[96,128]{1,0:T(8,128)S(1)} %collective-permute-done.2.xb, f32[96,128]{1,0:T(8,128)S(1)} %collective-permute-done.3.xa), custom_call_target="tpu_custom_call" | custom-call | flops 5734400 | bytes 2867200 | tf_op jit(solution)/shard_map/march/pallas_call | solution.py:559
  23.6 5.7 %all-to-all-done = f32[32,2,128]{2,1,0:T(2,128)S(1)} async-done(((f32[32,2,128]{2,1,0:T(2,128)}), f32[32,2,128]{2,1,0:T(2,128)S(1)}, u32[]{:S(2)}, u32[]{:S(2)}) %all-to-all-start) | async-done | bytes 32800 | tf_op jit(solution)/shard_map/all_to_all | solution.py:575
  29.3 0.7 %reduce_sum.9 = f32[2]{0:T(128)} reduce(f32[32,2,128]{2,1,0:T(2,128)S(1)} %all-to-all-done, f32[]{:T(128)} %constant.0.clone.1), dimensions={0,2}, to_apply=%region_0.0 | reduce | flops 8190 | bytes 32780 | tf_op jit(solution)/shard_map/reduce_sum | solution.py:576
Async XLA Ops:
  1.7 6.5 %collective-permute-start = (f32[128,128]{1,0:T(8,128)S(1)}, f32[128,128]{1,0:T(8,128)S(1)}, u32[]{:S(2)}, u32[]{:S(2)}) collective-permute-start(f32[128,128]{1,0:T(8,128)S(1)} %get-tuple-element.12), channel_id=1, source_target_pairs={{8,16},{16,8},{9,17},{17,9},{10,18},{18,10},{11,19},{19,11},{12,20... | collective-permute-start | bytes 196616 | tf_op jit(solution)/shard_map/ppermute | solution.py:501
  2.4 11.1 %copy-start = (bf16[3,3,14,16,128]{4,3,2,1,0:T(8,128)(2,1)S(1)}, bf16[3,3,14,16,128]{4,3,2,1,0:T(8,128)(2,1)}, u32[]{:S(2)}) copy-start(bf16[3,3,14,16,128]{4,3,2,1,0:T(8,128)(2,1)} %param.11) | copy-start | bytes 1548292
  2.4 11.1 %copy-start.1 = (s32[16,128]{1,0:T(8,128)S(1)}, s32[16,128]{1,0:T(8,128)}, u32[]{:S(2)}) copy-start(s32[16,128]{1,0:T(8,128)} %blocks.3) | copy-start | bytes 24580
  2.4 5.8 %collective-permute-start.1 = (f32[128,128]{1,0:T(8,128)S(1)}, f32[128,128]{1,0:T(8,128)S(1)}, u32[]{:S(2)}, u32[]{:S(2)}) collective-permute-start(f32[128,128]{1,0:T(8,128)S(1)} %get-tuple-element.13), channel_id=1, source_target_pairs={{0,8},{8,0},{16,24},{24,16},{1,9},{9,1},{17,25},{25,17},{2,10},{10... | collective-permute-start | bytes 196616 | tf_op jit(solution)/shard_map/ppermute | solution.py:502
  8.4 5.5 %collective-permute-start.2 = (f32[96,128]{1,0:T(8,128)S(1)}, f32[96,128]{1,0:T(8,128)S(1)}, u32[]{:S(2)}, u32[]{:S(2)}) collective-permute-start(f32[96,128]{1,0:T(8,128)S(1)} %get-tuple-element.15), channel_id=1, source_target_pairs={{1,2},{2,1},{3,4},{4,3},{5,6},{6,5},{9,10},{10,9},{11,12},{12,11},... | collective-permute-start | bytes 147464 | tf_op jit(solution)/shard_map/ppermute | solution.py:533
  9.1 6.5 %collective-permute-start.3 = (f32[96,128]{1,0:T(8,128)S(1)}, f32[96,128]{1,0:T(8,128)S(1)}, u32[]{:S(2)}, u32[]{:S(2)}) collective-permute-start(f32[96,128]{1,0:T(8,128)S(1)} %get-tuple-element.16), channel_id=1, source_target_pairs={{0,1},{1,0},{2,3},{3,2},{4,5},{5,4},{6,7},{7,6},{8,9},{9,8},{10,11... | collective-permute-start | bytes 147464 | tf_op jit(solution)/shard_map/ppermute | solution.py:534
  16.3 13.0 %all-to-all-start = ((f32[32,2,128]{2,1,0:T(2,128)}), f32[32,2,128]{2,1,0:T(2,128)S(1)}, u32[]{:S(2)}, u32[]{:S(2)}) async-start(f32[32,2,128]{2,1,0:T(2,128)} %bitcast.3), calls=%async_computation | async-start | bytes 65536 | tf_op jit(solution)/shard_map/all_to_all | solution.py:575

commit v4 on v3

--- a/solution.py
+++ b/solution.py
@@ -25,6 +25,7 @@
 
 VMEM = pl.BlockSpec(memory_space=pltpu.VMEM)
 HBM = pl.BlockSpec(memory_space=pltpu.HBM)
+ANY = pl.BlockSpec(memory_space=pl.ANY)
 
 
 def shape_of(rows, ny):
@@ -309,42 +310,7 @@
             edges[pl.ds((3 * side + c) * (nz + 2) + 1, nz), :] = part
 
 
-def edge_kernel(nz, nx, layers, work, partial, edges, blocks, xb, xa, sums):
-    tall, deep = nx * (nz + 2), nz + 2
-    row, first, last = masks(deep)
-    odd_x = jnp.broadcast_to(is_odd("xy"), row.shape)
-    own = jnp.logical_and(row > 0, row < deep - 1)
-    low_side = jnp.logical_and(own, jnp.broadcast_to(lax.axis_index("xy"), row.shape) > 0)
-
-    def slot(slots, field):
-        at = pl.ds(slots.index(field) * deep, deep)
-        return jnp.where(odd_x, xa[at, :], xb[at, :]), jnp.where(odd_x, xb[at, :], xa[at, :])
-
-    def prev_y(f):
-        return f - jnp.where(first, 0.0, pltpu.roll(f, 1, 1))
-
-    def factor(side, c):
-        return edges[pl.ds((3 * side + c) * deep, deep), :]
-
-    mag_y = slot(X_LOW, H1)[0] - work[pl.ds(V2 * tall, deep, stride=nx), :]
-    mag_z = slot(X_LOW, H2)[0] + work[pl.ds(V1 * tall, deep, stride=nx), :]
-    near = DT_STEP * (mag_y * factor(0, 2) - mag_z * factor(0, 1))
-    v_y, v_z = slot(X_HIGH, V1)[1], slot(X_HIGH, V2)[1]
-    far = DT_STEP * (
-        v_y * factor(1, 1)
-        + v_z * factor(1, 2)
-        - (prev_y(v_y) + (v_z - pltpu.roll(v_z, 1, 0))) * factor(1, 0)
-    )
-    near = jnp.sum(jnp.where(low_side, near, 0.0), axis=0, keepdims=True)
-    far = jnp.sum(jnp.where(own, far, 0.0), axis=0, keepdims=True)
-
-    ends = (near * (-1.0 / layers), far * (-1.0 / layers))
-    sums[...] = partial[...] + spread(ends, (0, nx // 4 - 1), blocks, sums.shape)
-
-
-def march_kernel(
-    nz, nx, work, zh, xb, xa, e_out, h_out, xh, out_e, out_h, sems
-):
+def march(nz, nx, work, zh, xb, xa, e_out, h_out, xh, out_e, out_h, sems):
     cells, tall, deep = nz * nx, nx * (nz + 2), nz + 2
     index_z, index_x = lax.axis_index("gz"), lax.axis_index("xy")
     odd_x = is_odd("xy")
@@ -453,6 +419,55 @@
             pltpu.make_async_copy(source.at[at, :], target.at[at, :], sems.at[k * 3 + c]).wait()
 
 
+def edge_kernel(
+    nz, nx, layers, work, zh, partial, edges, blocks, xb, xa, sums, e_out, h_out, *scratch
+):
+    tall, deep = nx * (nz + 2), nz + 2
+    row, first, last = masks(deep)
+    odd_x = jnp.broadcast_to(is_odd("xy"), row.shape)
+    own = jnp.logical_and(row > 0, row < deep - 1)
+    low_side = jnp.logical_and(own, jnp.broadcast_to(lax.axis_index("xy"), row.shape) > 0)
+
+    def slot(slots, field):
+        at = pl.ds(slots.index(field) * deep, deep)
+        return jnp.where(odd_x, xa[at, :], xb[at, :]), jnp.where(odd_x, xb[at, :], xa[at, :])
+
+    def prev_y(f):
+        return f - jnp.where(first, 0.0, pltpu.roll(f, 1, 1))
+
+    def factor(side, c):
+        return edges[pl.ds((3 * side + c) * deep, deep), :]
+
+    mag_y = slot(X_LOW, H1)[0] - work[pl.ds(V2 * tall, deep, stride=nx), :]
+    mag_z = slot(X_LOW, H2)[0] + work[pl.ds(V1 * tall, deep, stride=nx), :]
+    near = DT_STEP * (mag_y * factor(0, 2) - mag_z * factor(0, 1))
+    v_y, v_z = slot(X_HIGH, V1)[1], slot(X_HIGH, V2)[1]
+    far = DT_STEP * (
+        v_y * factor(1, 1)
+        + v_z * factor(1, 2)
+        - (prev_y(v_y) + (v_z - pltpu.roll(v_z, 1, 0))) * factor(1, 0)
+    )
+    near = jnp.sum(jnp.where(low_side, near, 0.0), axis=0, keepdims=True)
+    far = jnp.sum(jnp.where(own, far, 0.0), axis=0, keepdims=True)
+
+    ends = (near * (-1.0 / layers), far * (-1.0 / layers))
+    sums[...] = partial[...] + spread(ends, (0, nx // 4 - 1), blocks, sums.shape)
+
+    @pl.when(waits_long())
+    def _():
+        march(nz, nx, work, zh, xb, xa, e_out, h_out, *scratch)
+
+
+def late_kernel(nz, nx, work, zh, xb, xa, gathered, e_in, h_in, e_out, h_out, *scratch):
+    @pl.when(jnp.logical_not(waits_long()))
+    def _():
+        march(nz, nx, work, zh, xb, xa, e_out, h_out, *scratch)
+
+
+def waits_long():
+    return lax.axis_index("xy") * 8 < lax.axis_size("xy")
+
+
 def swap_pairs(count, offset):
     pairs = []
     for low in range(offset, count - 1, 2):
@@ -544,35 +559,38 @@
         name="interior",
     )(e_saved.reshape(-1, ny), work, zh, block_map)
 
-    sums = pl.pallas_call(
+    fields = (shape_of(3 * cells, ny), shape_of(3 * cells, ny))
+    scratch = [
+        pltpu.VMEM((10 * deep * 8, ny), f32),
+        pltpu.VMEM((3 * cells, ny), f32),
+        pltpu.VMEM((3 * cells, ny), f32),
+        pltpu.SemaphoreType.DMA((6,)),
+    ]
+    sums, field_e, field_h = pl.pallas_call(
         functools.partial(edge_kernel, nz, nx, nz * slabs),
-        out_shape=shape_of(blocks, ny),
-        in_specs=[VMEM] * 6,
-        out_specs=VMEM,
+        out_shape=(shape_of(blocks, ny),) + fields,
+        in_specs=[VMEM] * 7,
+        out_specs=(VMEM, HBM, HBM),
+        scratch_shapes=scratch,
         compiler_params=params,
         cost_estimate=estimate(4 * field, 4 * field),
         name="edges",
-    )(work, partial, edges, block_map, xb, xa)
+    )(work, zh, partial, edges, block_map, xb, xa)
 
     gathered = lax.all_to_all(sums, ("gz", "xy"), 0, 0, tiled=True)
 
     field_e, field_h = pl.pallas_call(
-        functools.partial(march_kernel, nz, nx),
-        out_shape=(shape_of(3 * cells, ny), shape_of(3 * cells, ny)),
-        in_specs=[VMEM] * 4,
+        functools.partial(late_kernel, nz, nx),
+        out_shape=fields,
+        in_specs=[VMEM] * 4 + [ANY, HBM, HBM],
         out_specs=(HBM, HBM),
-        scratch_shapes=[
-            pltpu.VMEM((10 * deep * 8, ny), f32),
-            pltpu.VMEM((3 * cells, ny), f32),
-            pltpu.VMEM((3 * cells, ny), f32),
-            pltpu.SemaphoreType.DMA((6,)),
-        ],
+        input_output_aliases={5: 0, 6: 1},
+        scratch_shapes=scratch,
         compiler_params=params,
         cost_estimate=estimate(200 * field, 4 * 25 * field),
-        name="march",
-    )(work, zh, xb, xa)
-
-    gathered = lax.all_to_all(sums, ("gz", "xy"), 0, 0, tiled=True)
+        name="fields",
+    )(work, zh, xb, xa, gathered, field_e, field_h)
+
     design_grad = jnp.sum(gathered.reshape(-1, B_DEV, ny), axis=(0, 2))
     return field_e.reshape(adjoint_e.shape), field_h.reshape(adjoint_h.shape), design_grad
 

time: 30.2 us -> 29.5 us (0.977)
  blocking collectives: 0 us -> 11.4 us
  starting transfers between devices: 15.9 us -> 10.1 us
  waiting for transfers between devices: 7.34 us -> 1.67 us
  Pallas kernels: 5.29 us -> 4.74 us
    all_to_all x0 -> x1, blocking collectives: none -> 11.4 us  [on_device(): gathered = lax.all_to_all(sums, ('gz', 'xy'), 0, 0, tiled=True)]
    all_to_all x1 -> x0, starting transfers between devices: 5.83 us -> none  [on_device(): gathered = lax.all_to_all(sums, ('gz', 'xy'), 0, 0, tiled=True)]
    all_to_all x1 -> x0, waiting for transfers between devices: 5.67 us -> none  [on_device(): gathered = lax.all_to_all(sums, ('gz', 'xy'), 0, 0, tiled=True)]
    pallas_call x1, Pallas kernels: 1.51 us -> 0.05 us  [on_device(): pl.pallas_call(functools.partial(late_kernel, nz, nx), out_shape=fields,...]
    pallas_call x1, Pallas kernels: 0.71 us -> 1.61 us  [on_device(): pl.pallas_call(functools.partial(edge_kernel, nz, nx, nz * slabs), out_sh...]
  transfers between devices with their start and end apart: 5 -> 4, of which waited for: 2 -> 1; matrix products, arithmetic and copies ran while one was open for 0% -> 0% of each run, Pallas kernels for 11% -> 6%
where the time goes in v4:
time: 29.5 us; the launch traced here: 29.2 us
  blocking collectives  11.4 us (39%)
  starting transfers between devices  10.1 us (34%)
  Pallas kernels  4.74 us (16%)
  waiting for transfers between devices  1.67 us (6%)
  between operations  0.73 us (2%)
  other arithmetic  0.66 us (2%)
    all_to_all x1, blocking collectives, on_device(): gathered = lax.all_to_all(sums, ('gz', 'xy'), 0, 0, tiled=True)  11.4 us
    ppermute x1, starting transfers between devices, on_device(): xa = lax.ppermute(xa, 'xy', swap_pairs(tiles, 0))  4.38 us
    ppermute x1, starting transfers between devices, on_device(): za = lax.ppermute(za, 'gz', swap_pairs(slabs, 0))  4.36 us
    ppermute x1, waiting for transfers between devices, on_device(): xa = lax.ppermute(xa, 'xy', swap_pairs(tiles, 0))  1.67 us
    pallas_call x1, Pallas kernels, on_device(): pl.pallas_call(functools.partial(edge_kernel, nz, nx, nz * slabs), out_sh...  1.61 us
    pallas_call x1, Pallas kernels, on_device(): pl.pallas_call(functools.partial(prepare_kernel, nz, nx), out_shape=shape...  1.41 us
    pallas_call x1, Pallas kernels, on_device(): pl.pallas_call(functools.partial(faces_kernel, nz, nx), out_shape=(z_msg,...  1.1 us
    ppermute x1, starting transfers between devices, on_device(): zb = lax.ppermute(zb, 'gz', swap_pairs(slabs, 1))  0.66 us
  transfers between devices with their start and end apart: 4, of which 1 were waited for; matrix products, arithmetic and copies ran while one was open for 0% of the time, Pallas kernels for 6%

profile of v4, /device:TPU:0, one launch (start us, length us, event | category | flops | bytes accessed | tf_op | source)
XLA Modules:
  0.0 29.2 jit_solution(5805011155122144141)
XLA Ops:
  0.6 1.1 %faces.1 = (f32[128,128]{1,0:T(8,128)S(1)}, f32[128,128]{1,0:T(8,128)S(1)}) custom-call(f32[8]{0:T(128)} %eps_in.3, f32[3,14,16,128]{3,2,1,0:T(8,128)} %e_in.3, f32[3,14,16,128]{3,2,1,0:T(8,128)} %h_in.3, bf16[3,14,16,128]{3,2,1,0:T(8,128)(2,1)} %s_in.3, s32[14,16,128]{2,1,0:T(8,128)} %mat_in.3, s32[14,16,128]{2,1,0:T(8,128)} %pml_in.3), custom_call_target="tpu_custom_call" | custom-call | flops 430080 | bytes 458752 | tf_op jit(solution)/shard_map/faces/pallas_call | solution.py:497
  1.7 0.7 %collective-permute-start = (f32[128,128]{1,0:T(8,128)S(1)}, f32[128,128]{1,0:T(8,128)S(1)}, u32[]{:S(2)}, u32[]{:S(2)}) collective-permute-start(f32[128,128]{1,0:T(8,128)S(1)} %get-tuple-element.15), channel_id=1, source_target_pairs={{8,16},{16,8},{9,17},{17,9},{10,18},{18,10},{11,19},{19,11},{12,20... | collective-permute-start | bytes 196616 | tf_op jit(solution)/shard_map/ppermute | solution.py:516
  2.4 0.0 copy-start
  2.4 0.0 copy-start.1
  2.4 4.4 %collective-permute-start.1 = (f32[128,128]{1,0:T(8,128)S(1)}, f32[128,128]{1,0:T(8,128)S(1)}, u32[]{:S(2)}, u32[]{:S(2)}) collective-permute-start(f32[128,128]{1,0:T(8,128)S(1)} %get-tuple-element.16), channel_id=1, source_target_pairs={{0,8},{8,0},{16,24},{24,16},{1,9},{9,1},{17,25},{25,17},{2,10},{10... | collective-permute-start | bytes 196616 | tf_op jit(solution)/shard_map/ppermute | solution.py:517
  6.8 1.4 %prepare.1.work = f32[3840,128]{1,0:T(8,128)S(1)} custom-call(f32[8]{0:T(128)} %eps_in.3, f32[3,14,16,128]{3,2,1,0:T(8,128)} %e_in.3, f32[3,14,16,128]{3,2,1,0:T(8,128)} %h_in.3, bf16[3,14,16,128]{3,2,1,0:T(8,128)(2,1)} %s_in.3, s32[14,16,128]{2,1,0:T(8,128)} %mat_in.3, s32[14,16,128]{2,1,0:T(8,128)} %pml_in.3), custom_call_target="tpu_custom_call" | custom-call | flops 2293760 | bytes 2867200 | tf_op jit(solution)/shard_map/prepare/pallas_call | solution.py:519
  8.2 0.0 collective-permute-done.zb
  8.2 0.0 collective-permute-done.1.za
  8.2 0.2 columns.1
  8.4 0.7 %collective-permute-start.2 = (f32[96,128]{1,0:T(8,128)S(1)}, f32[96,128]{1,0:T(8,128)S(1)}, u32[]{:S(2)}, u32[]{:S(2)}) collective-permute-start(f32[96,128]{1,0:T(8,128)S(1)} %get-tuple-element.18), channel_id=1, source_target_pairs={{1,2},{2,1},{3,4},{4,3},{5,6},{6,5},{9,10},{10,9},{11,12},{12,11},... | collective-permute-start | bytes 147464 | tf_op jit(solution)/shard_map/ppermute | solution.py:548
  9.1 4.4 %collective-permute-start.3 = (f32[96,128]{1,0:T(8,128)S(1)}, f32[96,128]{1,0:T(8,128)S(1)}, u32[]{:S(2)}, u32[]{:S(2)}) collective-permute-start(f32[96,128]{1,0:T(8,128)S(1)} %get-tuple-element.19), channel_id=1, source_target_pairs={{0,1},{1,0},{2,3},{3,2},{4,5},{5,4},{6,7},{7,6},{8,9},{9,8},{10,11... | collective-permute-start | bytes 147464 | tf_op jit(solution)/shard_map/ppermute | solution.py:549
  13.5 0.0 copy-done
  13.5 0.0 copy-done.1
  13.5 0.4 %interior.1 = (f32[64,128]{1,0:T(8,128)S(1)}, f32[96,128]{1,0:T(8,128)S(1)}) custom-call(bf16[2016,128]{1,0:T(8,128)(2,1)S(1)} %bitcast.5, f32[3840,128]{1,0:T(8,128)S(1)} %prepare.1.work, f32[328,128]{1,0:T(8,128)S(1)} %get-tuple-element.17.zh, s32[16,128]{1,0:T(8,128)S(1)} %copy-done.1), custom_call_target="tpu_custom_call" | custom-call | flops 4300800 | bytes 2293760 | tf_op jit(solution)/shard_map/interior/pallas_call | solution.py:551
  13.9 0.0 collective-permute-done.2.xb
  13.9 1.7 %collective-permute-done.3.xa = f32[96,128]{1,0:T(8,128)S(1)} collective-permute-done((f32[96,128]{1,0:T(8,128)S(1)}, f32[96,128]{1,0:T(8,128)S(1)}, u32[]{:S(2)}, u32[]{:S(2)}) %collective-permute-start.3) | collective-permute-done | bytes 49184 | tf_op jit(solution)/shard_map/ppermute | solution.py:549
  15.5 1.6 %edges.1 = (f32[64,128]{1,0:T(8,128)S(1)}, f32[672,128]{1,0:T(8,128)}, f32[672,128]{1,0:T(8,128)}) custom-call(f32[3840,128]{1,0:T(8,128)S(1)} %prepare.1.work, f32[328,128]{1,0:T(8,128)S(1)} %get-tuple-element.17.zh, f32[64,128]{1,0:T(8,128)S(1)} %get-tuple-element.20.partial, f32[96,128]{1,0:T(8,128)S(1)} %get-tuple-element.21.edges, ...), custom_call_target="tpu_custom_call" | custom-call | flops 114688 | bytes 114688 | tf_op jit(solution)/shard_map/edges/pallas_call | solution.py:569
  17.2 11.4 %all_to_all.11 = f32[32,2,128]{2,1,0:T(2,128)S(1)} all-to-all(f32[32,2,128]{2,1,0:T(2,128)S(1)} %bitcast.7), channel_id=1, replica_groups=mesh['gz'=4,'xy'=8] {'gz','xy'}, dimensions={0} | all-to-all | bytes 65536 | tf_op jit(solution)/shard_map/all_to_all | solution.py:580
  28.5 0.7 %reduce_sum.9 = f32[2]{0:T(128)} reduce(f32[32,2,128]{2,1,0:T(2,128)S(1)} %all_to_all.11, f32[]{:T(128)} %constant.0.clone.1), dimensions={0,2}, to_apply=%region_0.0 | reduce | flops 8190 | bytes 32780 | tf_op jit(solution)/shard_map/reduce_sum | solution.py:594
  29.2 0.1 fields.1
Async XLA Ops:
  1.7 6.5 %collective-permute-start = (f32[128,128]{1,0:T(8,128)S(1)}, f32[128,128]{1,0:T(8,128)S(1)}, u32[]{:S(2)}, u32[]{:S(2)}) collective-permute-start(f32[128,128]{1,0:T(8,128)S(1)} %get-tuple-element.15), channel_id=1, source_target_pairs={{8,16},{16,8},{9,17},{17,9},{10,18},{18,10},{11,19},{19,11},{12,20... | collective-permute-start | bytes 196616 | tf_op jit(solution)/shard_map/ppermute | solution.py:516
  2.4 11.1 %copy-start = (bf16[3,3,14,16,128]{4,3,2,1,0:T(8,128)(2,1)S(1)}, bf16[3,3,14,16,128]{4,3,2,1,0:T(8,128)(2,1)}, u32[]{:S(2)}) copy-start(bf16[3,3,14,16,128]{4,3,2,1,0:T(8,128)(2,1)} %param.11) | copy-start | bytes 1548292
  2.4 11.1 %copy-start.1 = (s32[16,128]{1,0:T(8,128)S(1)}, s32[16,128]{1,0:T(8,128)}, u32[]{:S(2)}) copy-start(s32[16,128]{1,0:T(8,128)} %blocks.3) | copy-start | bytes 24580
  2.4 5.8 %collective-permute-start.1 = (f32[128,128]{1,0:T(8,128)S(1)}, f32[128,128]{1,0:T(8,128)S(1)}, u32[]{:S(2)}, u32[]{:S(2)}) collective-permute-start(f32[128,128]{1,0:T(8,128)S(1)} %get-tuple-element.16), channel_id=1, source_target_pairs={{0,8},{8,0},{16,24},{24,16},{1,9},{9,1},{17,25},{25,17},{2,10},{10... | collective-permute-start | bytes 196616 | tf_op jit(solution)/shard_map/ppermute | solution.py:517
  8.4 5.5 %collective-permute-start.2 = (f32[96,128]{1,0:T(8,128)S(1)}, f32[96,128]{1,0:T(8,128)S(1)}, u32[]{:S(2)}, u32[]{:S(2)}) collective-permute-start(f32[96,128]{1,0:T(8,128)S(1)} %get-tuple-element.18), channel_id=1, source_target_pairs={{1,2},{2,1},{3,4},{4,3},{5,6},{6,5},{9,10},{10,9},{11,12},{12,11},... | collective-permute-start | bytes 147464 | tf_op jit(solution)/shard_map/ppermute | solution.py:548
  9.1 6.5 %collective-permute-start.3 = (f32[96,128]{1,0:T(8,128)S(1)}, f32[96,128]{1,0:T(8,128)S(1)}, u32[]{:S(2)}, u32[]{:S(2)}) collective-permute-start(f32[96,128]{1,0:T(8,128)S(1)} %get-tuple-element.19), channel_id=1, source_target_pairs={{0,1},{1,0},{2,3},{3,2},{4,5},{5,4},{6,7},{7,6},{8,9},{9,8},{10,11... | collective-permute-start | bytes 147464 | tf_op jit(solution)/shard_map/ppermute | solution.py:549
